TPU v7x, 256 devices: a whole 4x4x8 slice. The times are simulated.
256 devices in a mesh: rows: 256 (over y, x, z, core).
Axes of the slice: x: 4, y: 4, z: 8, core: 2. Of those that a mesh axis runs over, the one named last changes fastest.
Arguments:
- embed: float32 [1048576, 64], P('rows'), may hold values from -6 to 6
- amplitude: float32 [1048576], P('rows'), may hold values from 0.4 to 4.3, as said below
- pivots: int32 [4, 128], replicated, may hold values from 0 to 1048575, as said below
Outputs:
- factor: float32 [1048576, 512], P('rows')
- residual: float32 [1048576], P('rows')
- means: float32 [4], replicated
Inputs may be any that keep to these rules, and one draw needn't show every extreme that they name: `pivots`: global point ids; all 512 ids are distinct. Within one panel at most 2 ids lie on one device (a block of 4096 consecutive ids), and in every panel some device holds exactly 2. `amplitude`: Positive.
All inputs are finite; a program needn't handle non-finite values.
Results may differ from a plain program's by a relative error of at most 0.0003.
Values sent between devices are 32-bit elements; how exact they have to be, the bound alone decides.
A program may use at most 128 MiB of HBM per device.

v0:
```python
import jax
import jax.numpy as jnp
from jax import lax
from jax.sharding import PartitionSpec as P


def kernel_block(left, left_amp, left_sq, right, right_amp, right_sq, width):
    inner = jnp.dot(
        left, right.T, precision=lax.Precision.HIGHEST, preferred_element_type=jnp.float32
    )
    dist = jnp.maximum(left_sq[:, None] + right_sq[None, :] - 2.0 * inner, 0.0)
    return left_amp[:, None] * right_amp[None, :] * jnp.exp(-dist / width)


def lower_inverse(block):
    lower = jnp.linalg.cholesky(0.5 * (block + block.T))
    ident = jnp.eye(block.shape[0], dtype=block.dtype)
    return lax.linalg.triangular_solve(lower, ident, left_side=True, lower=True)


def slots_within(owners, panel_width):
    order = jnp.arange(panel_width, dtype=jnp.int32)
    earlier = (owners[:, None] == owners[None, :]) & (order[None, :] < order[:, None])
    return jnp.sum(earlier.astype(jnp.int32), axis=1)


def local(embed, amplitude, pivots):
    local_rows = embed.shape[0]
    feature_count = embed.shape[1]
    panel_count = pivots.shape[0]
    panel_width = pivots.shape[1]
    devices = lax.axis_size("rows")
    position = lax.axis_index("rows")
    slot_count = max(2, 256 // devices)
    squared = jnp.sum(embed * embed, axis=1)
    residual = amplitude * amplitude
    columns = []
    partial_sums = []
    for panel in range(panel_count):
        pivot_ids = pivots[panel]
        owners = pivot_ids // local_rows
        offsets = pivot_ids % local_rows
        mine = owners == position
        if columns:
            factor = jnp.concatenate(columns, axis=1)
            source = jnp.concatenate([embed, factor], axis=1)
        else:
            source = embed
        taken = jnp.take(source, offsets, axis=0)
        taken_amp = jnp.take(amplitude, offsets, axis=0)
        slot_of = slots_within(owners, panel_width)
        placing = (
            (slot_of[None, :] == jnp.arange(slot_count, dtype=jnp.int32)[:, None]) & mine[None, :]
        ).astype(jnp.float32)
        packed = jnp.dot(
            placing, taken, precision=lax.Precision.HIGHEST, preferred_element_type=jnp.float32
        )
        packed_amp = jnp.dot(
            placing, taken_amp, precision=lax.Precision.HIGHEST, preferred_element_type=jnp.float32
        )
        whole, whole_amp = (
            lax.all_gather(packed, "rows", axis=0, tiled=True),
            lax.all_gather(packed_amp, "rows", axis=0, tiled=True),
        )
        where_from = owners * slot_count + slot_of
        chosen_all = jnp.take(whole, where_from, axis=0)
        chosen_amp = jnp.take(whole_amp, where_from, axis=0)
        chosen = chosen_all[:, :feature_count]
        chosen_sq = jnp.sum(chosen * chosen, axis=1)
        cross = kernel_block(
            embed, amplitude, squared, chosen, chosen_amp, chosen_sq, feature_count
        )
        block = kernel_block(
            chosen, chosen_amp, chosen_sq, chosen, chosen_amp, chosen_sq, feature_count
        )
        if columns:
            chosen_rows = chosen_all[:, feature_count:]
            cross = cross - jnp.dot(
                factor,
                chosen_rows.T,
                precision=lax.Precision.HIGHEST,
                preferred_element_type=jnp.float32,
            )
            block = block - jnp.dot(
                chosen_rows,
                chosen_rows.T,
                precision=lax.Precision.HIGHEST,
                preferred_element_type=jnp.float32,
            )
        inverse = lower_inverse(block)
        fresh = jnp.dot(
            cross, inverse.T, precision=lax.Precision.HIGHEST, preferred_element_type=jnp.float32
        )
        columns.append(fresh)
        residual = residual - jnp.sum(fresh * fresh, axis=1)
        partial_sums.append(jnp.sum(residual))
    totals = lax.psum(jnp.stack(partial_sums), "rows")
    means = totals / (local_rows * devices)
    return (jnp.concatenate(columns, axis=1), residual, means)


def solution(mesh):
    return jax.shard_map(
        local,
        mesh=mesh,
        in_specs=(P("rows", None), P("rows"), P()),
        out_specs=(P("rows", None), P("rows"), P()),
        check_vma=False,
    )
```

profile of v0, /device:TPU:1, one launch (start us, length us, event | category | flops | bytes accessed | tf_op | source)
XLA Modules:
  0.0 683.3 jit_solution(2128310664968788016)
XLA Ops:
  5.6 1.8 copy.60
  8.3 67.0 %all-gather = f32[256,2,64]{2,1,0:T(2,128)S(1)} all-gather(f32[1,2,64]{2,1,0:T(2,128)S(1)} %convolution_bitcast_fusion.3), channel_id=1, replica_groups=mesh['rows'=256] {'rows'}, dimensions={0}, use_global_device_ids=true | all-gather | bytes 131584 | tf_op jit(solution)/shard_map/all_gather | solution.py:62
  82.5 74.2 %all-reduce.4 = (f32[512]{0:T(512)S(1)}, f32[512]{0:T(512)S(1)}, f32[512]{0:T(512)S(1)}, f32[512]{0:T(512)S(1)}) all-reduce(f32[512]{0:T(512)S(1)} %dynamic-update-slice.2, f32[512]{0:T(512)S(1)} %dynamic-update-slice.3, f32[512]{0:T(512)S(1)} %dynamic-update-slice.4, f32[512]{0:T(512)S(1)} %dynamic-update-slice.5), channel_id=1, replica_groups=mesh['rows'=256] {'rows'}, use_global_device_ids=true, to_apply=%add | all-reduce | flops 2048 | bytes 16384
  158.2 11.7 %cholesky.74 = f32[128,128]{1,0:T(8,128)S(1)} custom-call(f32[128,128]{1,0:T(8,128)S(1)} %fusion.113), custom_call_target="Cholesky" | custom-call | tf_op jit(solution)/shard_map/jit(cholesky)/cholesky | solution.py:16
  171.3 9.8 %custom-call.8 = f32[1,128,128]{1,2,0:T(8,128)S(1)} custom-call(f32[1,128,128]{2,1,0:T(8,128)S(1)} %fusion.59), custom_call_target="InvertDiagBlocksLowerTriangular" | custom-call | tf_op jit(solution)/shard_map/triangular_solve/custom-call.0 | solution.py:18
  181.5 2.4 fusion.34
  183.9 2.1 multiply_reduce_fusion.3
  185.9 2.0 pad_maximum_fusion.3
  187.9 5.1 copy.63
  193.0 2.9 gather_fusion.2
  196.2 72.4 %all-gather.1 = f32[256,2,192]{2,1,0:T(2,128)} all-gather(f32[1,2,192]{2,1,0:T(2,128)S(1)} %convolution_bitcast_fusion.2), channel_id=1, replica_groups=mesh['rows'=256] {'rows'}, dimensions={0}, use_global_device_ids=true | all-gather | bytes 394752 | tf_op jit(solution)/shard_map/all_gather | solution.py:62
  268.6 2.2 reshape.810
  270.8 1.8 gather_fusion.3
  276.0 10.1 %gather_fusion.11 = f32[128]{0:T(128)S(1)} fusion(f32[512]{0:T(512)S(1)} %get-tuple-element.22, s32[1024]{0:T(1024)S(1)} %pad_clamp_fusion.10), kind=kCustom, calls=%fused_computation.5.clone | custom fusion | bytes 1536 | tf_op jit(solution)/shard_map/jit(_take)/gather | solution.py:67
  287.9 11.7 %cholesky.85 = f32[128,128]{1,0:T(8,128)S(1)} custom-call(f32[128,128]{1,0:T(8,128)S(1)} %fusion.111), custom_call_target="Cholesky" | custom-call | tf_op jit(solution)/shard_map/jit(cholesky)/cholesky | solution.py:16
  300.9 9.8 %custom-call.9 = f32[1,128,128]{1,2,0:T(8,128)S(1)} custom-call(f32[1,128,128]{2,1,0:T(8,128)S(1)} %fusion.60), custom_call_target="InvertDiagBlocksLowerTriangular" | custom-call | tf_op jit(solution)/shard_map/triangular_solve/custom-call.0 | solution.py:18
  311.0 2.3 fusion.27
  313.4 2.0 convolution_subtract_fusion.1
  315.4 2.9 multiply_reduce_fusion.2
  319.8 2.9 pad_maximum_fusion.2
  322.7 6.3 copy.68
  329.0 3.6 gather_fusion.4
  332.9 77.6 %all-gather.2 = f32[256,2,320]{2,1,0:T(2,128)} all-gather(f32[1,2,320]{2,1,0:T(2,128)S(1)} %convolution_bitcast_fusion.1), channel_id=1, replica_groups=mesh['rows'=256] {'rows'}, dimensions={0}, use_global_device_ids=true | all-gather | bytes 657920 | tf_op jit(solution)/shard_map/all_gather | solution.py:62
  410.5 2.6 reshape.812
  413.1 2.6 gather_fusion.5
  422.6 12.5 %cholesky.96 = f32[128,128]{1,0:T(8,128)S(1)} custom-call(f32[128,128]{1,0:T(8,128)} %fusion.109), custom_call_target="Cholesky" | custom-call | tf_op jit(solution)/shard_map/jit(cholesky)/cholesky | solution.py:16
  436.5 9.8 %custom-call.10 = f32[1,128,128]{1,2,0:T(8,128)S(1)} custom-call(f32[1,128,128]{2,1,0:T(8,128)S(1)} %fusion.61), custom_call_target="InvertDiagBlocksLowerTriangular" | custom-call | tf_op jit(solution)/shard_map/triangular_solve/custom-call.0 | solution.py:18
  446.6 2.3 fusion.20
  449.0 2.5 convolution_subtract_fusion
  451.5 2.5 multiply_reduce_fusion.1
  455.4 3.3 pad_maximum_fusion.1
  458.7 8.9 %copy.73 = f32[4096,448]{1,0:T(8,128)} copy(f32[4096,448]{0,1:T(8,128)} %pad_maximum_fusion.1) | data formatting | bytes 14680064 | tf_op jit(solution)/shard_map/concatenate | solution.py:46
  467.6 4.3 gather_fusion.6
  472.2 64.8 %all-gather.3 = f32[256,2,448]{2,1,0:T(2,128)} all-gather(f32[1,2,448]{2,1,0:T(2,128)S(1)} %convolution_bitcast_fusion), channel_id=1, replica_groups=mesh['rows'=256] {'rows'}, dimensions={0}, use_global_device_ids=true | all-gather | bytes 921088 | tf_op jit(solution)/shard_map/all_gather | solution.py:62
  537.0 2.9 reshape.814
  539.9 2.8 gather_fusion.7
  544.8 1.6 copy.75
  548.3 1.4 gather_fusion.15
  551.6 1.5 fusion.103
  553.0 12.5 %cholesky.107 = f32[128,128]{1,0:T(8,128)S(1)} custom-call(f32[128,128]{1,0:T(8,128)} %fusion.103), custom_call_target="Cholesky" | custom-call | tf_op jit(solution)/shard_map/jit(cholesky)/cholesky | solution.py:16
  567.5 10.6 %custom-call.11 = f32[1,128,128]{1,2,0:T(8,128)S(1)} custom-call(f32[1,128,128]{2,1,0:T(8,128)} %fusion.62), custom_call_target="InvertDiagBlocksLowerTriangular" | custom-call | tf_op jit(solution)/shard_map/triangular_solve/custom-call.0 | solution.py:18
  578.5 6.3 fusion
  584.8 2.4 fusion.13
  587.2 3.4 multiply_reduce_fusion
  591.8 2.7 pad_maximum_fusion.4
  594.4 73.4 %psum.7 = f32[4]{0:T(128)S(1)} all-reduce(f32[4]{0:T(128)S(1)} %pad_maximum_fusion.4), channel_id=1, replica_groups=mesh['rows'=256] {'rows'}, use_global_device_ids=true, to_apply=%region_19.24 | all-reduce | flops 4 | bytes 32 | tf_op jit(solution)/shard_map/psum | solution.py:97
  668.3 5.8 pad_maximum_fusion
  674.1 8.9 %copy.79 = f32[4096,512]{1,0:T(8,128)} copy(f32[4096,512]{0,1:T(8,128)} %pad_maximum_fusion) | data formatting | bytes 16777216
  (152 shorter events, 44.7 us)
Async XLA Ops:
  2.9 73.0 %copy-start.9 = (s32[128]{0:T(128)}, s32[128]{0:T(128)S(1)}, u32[]{:S(2)}) copy-start(s32[128]{0:T(128)S(1)} %get-tuple-element.85) | copy-start | bytes 1540
  3.7 75.5 %copy-start.15 = (pred[128]{0:T(512)(128)(4,1)}, pred[128]{0:T(512)(128)(4,1)S(1)}, u32[]{:S(2)}) copy-start(pred[128]{0:T(512)(128)(4,1)S(1)} %get-tuple-element.81) | copy-start | bytes 388
  3.7 76.9 %copy-start.13 = (pred[128]{0:T(512)(128)(4,1)}, pred[128]{0:T(512)(128)(4,1)S(1)}, u32[]{:S(2)}) copy-start(pred[128]{0:T(512)(128)(4,1)S(1)} %get-tuple-element.49) | copy-start | bytes 388
  5.6 71.0 %copy-start = (f32[4096]{0:T(1024)S(1)}, f32[4096]{0:T(1024)}, u32[]{:S(2)}) copy-start(f32[4096]{0:T(1024)} %param.11) | copy-start | bytes 49156
  75.9 105.5 %copy-start.3 = (f32[4096,64]{0,1:T(8,128)S(1)}, f32[4096,64]{0,1:T(8,128)}, u32[]{:S(2)}) copy-start(f32[4096,64]{0,1:T(8,128)} %param.10) | copy-start | bytes 3145732
  318.4 1.4 copy-start.1
  322.7 6.3 copy-start.20
  322.7 10.0 %copy-start.12 = (pred[128]{0:T(512)(128)(4,1)S(1)}, pred[128]{0:T(512)(128)(4,1)}, u32[]{:S(2)}) copy-start(pred[128]{0:T(512)(128)(4,1)} %get-tuple-element.76) | copy-start | bytes 388
  322.7 10.0 %copy-start.16 = (pred[128]{0:T(512)(128)(4,1)S(1)}, pred[128]{0:T(512)(128)(4,1)}, u32[]{:S(2)}) copy-start(pred[128]{0:T(512)(128)(4,1)} %copy-done.15) | copy-start | bytes 388
  329.0 84.1 %copy-start.18 = (s32[128]{0:T(128)S(1)}, s32[128]{0:T(128)}, u32[]{:S(2)}) copy-start(s32[128]{0:T(128)} %get-tuple-element.66) | copy-start | bytes 1540
  332.9 82.8 %copy-start.10 = (s32[128]{0:T(128)S(1)}, s32[128]{0:T(128)}, u32[]{:S(2)}) copy-start(s32[128]{0:T(128)} %copy-done.9) | copy-start | bytes 1540
  417.0 0.6 copy-start.5
  446.6 2.4 copy-start.2
  451.5 2.5 copy-start.7
  454.0 1.4 copy-start.4
  458.7 8.9 %copy-start.19 = (s32[128,1]{0,1:T(1,128)S(1)}, s32[128,1]{0,1:T(1,128)}, u32[]{:S(2)}) copy-start(s32[128,1]{0,1:T(1,128)} %get-tuple-element.31) | copy-start | bytes 1540
  467.6 4.3 copy-start.11
  467.6 4.3 copy-start.14
  471.9 68.0 %copy-start.17 = (s32[128]{0:T(128)S(1)}, s32[128]{0:T(128)}, u32[]{:S(2)}) copy-start(s32[128]{0:T(128)} %get-tuple-element.30) | copy-start | bytes 1540
  547.5 2.2 copy-start.6
  587.2 3.4 copy-start.8
where the time goes:
time: 689 us; the launch traced here: 683 us
  blocking collectives  429 us (62%)
  other arithmetic  129 us (19%)
  local copies, waits for them, and re-layouts  86.6 us (13%)
  matrix products  36.7 us (5%)
    all_gather x4, blocking collectives, local(): lax.all_gather(packed, 'rows', axis=0, tiled=True)  282 us
    unnamed x1, blocking collectives  74.2 us
    psum x1, blocking collectives, local(): totals = lax.psum(jnp.stack(partial_sums), 'rows')  73.4 us
    another operation x12, other arithmetic, lower_inverse(): lower = jnp.linalg.cholesky(0.5 * (block + block.T))  51.2 us
    another operation x8, other arithmetic, lower_inverse(): return lax.linalg.triangular_solve(lower, ident, left_side=True, lower=True)  43.3 us
    unnamed x55, local copies, waits for them, and re-layouts  21.3 us
    concatenate x3, local copies, waits for them, and re-layouts, local(): source = jnp.concatenate([embed, factor], axis=1)  20.3 us
    gather x4, local copies, waits for them, and re-layouts, local(): chosen_amp = jnp.take(whole_amp, where_from, axis=0)  14.1 us

commit v1 on v0

v1 whole, which is shorter than its diff:
```python
import functools

import jax
import jax.numpy as jnp
from jax import lax
from jax.experimental import pallas as pl
from jax.experimental.pallas import tpu as pltpu
from jax.sharding import PartitionSpec as P
HI = lax.Precision.HIGHEST
F32 = jnp.float32

def spread_row(block, row):
    return jnp.broadcast_to(block[row:row+1, :], (8, 128))

def spread_col(block, col):
    return jnp.broadcast_to(block[:, col:col+1], (8, 128))

def eliminate(blocks, lookahead=True):
    lane = lax.broadcasted_iota(jnp.int32, (8, 128), 1)
    sub = lax.broadcasted_iota(jnp.int32, (8, 128), 0)
    n = len(blocks)
    blocks = list(blocks)
    diag = [spread_col(blocks[0], k) for k in range(8)]
    for j in range(n):
        inside = (lane >= 8 * j) & (lane < 8 * j + 8)
        below = {b: [spread_col(blocks[b], 8 * j + k) for k in range(8)] for b in range(j + 1, n)}
        nxt = [spread_col(blocks[j + 1], 8 * (j + 1) + k) for k in range(8)] if j + 1 < n else None
        rest = jnp.where(inside, jnp.where(lane - 8 * j == sub, 1.0, 0.0), blocks[j])
        rows = []
        for k in range(8):
            scale = lax.rsqrt(spread_row(diag[k], k))
            low = diag[k] * scale
            row = spread_row(rest, k) * scale
            rows.append(row)
            if k < 7:
                rest = rest - low * row
            for b in below:
                below[b][k] = below[b][k] * scale
            for m in range(k + 1, 8):
                factor = spread_row(low, m)
                diag[m] = diag[m] - low * factor
                for b in below:
                    below[b][m] = below[b][m] - below[b][k] * factor
        out = rows[0]
        for k in range(1, 8):
            out = jnp.where(sub == k, rows[k], out)
        blocks[j] = out
        if j + 1 < n:
            w = below[j + 1]
            for k in range(8):
                t = [w[l] * spread_row(w[l], k) for l in range(8)]
                t = ((t[0] + t[1]) + (t[2] + t[3])) + ((t[4] + t[5]) + (t[6] + t[7]))
                nxt[k] = nxt[k] - t
            diag = nxt
        for b in below:
            t = [below[b][l] * rows[l] for l in range(8)]
            t = ((t[0] + t[1]) + (t[2] + t[3])) + ((t[4] + t[5]) + (t[6] + t[7]))
            blocks[b] = jnp.where(inside, 0.0, blocks[b]) - t
    return blocks

def lower_inverse_512(a_ref, store):
    lane = lax.broadcasted_iota(jnp.int32, (128, 128), 1)
    sub = lax.broadcasted_iota(jnp.int32, (128, 128), 0)
    size = a_ref.shape[0]
    panels = size // 128
    for p in range(panels):
        lo = 128 * p
        got = eliminate([a_ref[lo + 8 * b: lo + 8 * b + 8, lo:lo + 128] for b in range(16)])
        inv = jnp.where(lane <= sub, jnp.concatenate(got, axis=0), 0.0)
        right = None
        if p + 1 < panels:
            right = jnp.dot(inv, a_ref[lo:lo + 128, lo + 128:], precision=HI, preferred_element_type=F32)
            a_ref[lo + 128:, lo + 128:] -= lax.dot_general(right, right, (((0,), (0,)), ((), ())), precision=HI, preferred_element_type=F32)
        left = inv
        if p:
            left = jnp.concatenate([jnp.dot(inv, a_ref[lo:lo + 128, :lo], precision=HI, preferred_element_type=F32), inv], axis=1)
        store(p, left)
        if p + 1 < panels:
            upd = lax.dot_general(right, left, (((0,), (0,)), ((), ())), precision=HI, preferred_element_type=F32)
            if p:
                a_ref[lo + 128:, :lo] -= upd[:, :lo]
            a_ref[lo + 128:, lo:lo + 128] = -upd[:, lo:]

LOG2E = 1.4426950408889634
MESH = pl.DeviceIdType.MESH
BF16 = jnp.bfloat16


def split_two(value):
    high = value.astype(BF16)
    return high, (value - high.astype(F32)).astype(BF16)


def split_three(value):
    high = value.astype(BF16)
    left = value - high.astype(F32)
    middle = left.astype(BF16)
    return high, middle, (left - middle.astype(F32)).astype(BF16)


def place():
    me = lax.axis_index("rows")
    core = lax.rem(me, 2)
    deep = lax.rem(me // 2, 8)
    plane = me // 16
    return me, core, deep, plane


def device_of(plane, deep, core):
    return (plane * 8 + deep) * 2 + core


def features_of(embed_ref, amp_ref, first):
    part = embed_ref[:, first:first + 128]
    amp = amp_ref[first // 128:first // 128 + 1, :]
    squared = jnp.sum(part * part, axis=0, keepdims=True) * (LOG2E / 64)
    high, low = split_two(part)
    high, low = high.astype(F32), low.astype(F32)
    ones = jnp.ones((1, 128), F32)
    extra = [v.astype(F32) for v in split_three(squared)] + [ones] * 3 + [v.astype(F32) for v in split_three(amp)]
    row = lax.broadcasted_iota(jnp.int32, (64, 128), 0)
    tail = jnp.zeros((64, 128), F32)
    for index, value in enumerate(extra):
        tail = jnp.where(row == index, value, tail)
    one = jnp.concatenate([high, low], axis=0).T.astype(BF16)
    two = jnp.concatenate([high, tail], axis=0).T.astype(BF16)
    return one, two


def gather_kernel(pivots_ref, embed_ref, amp_ref, features_ref, chosen_ref,
                  own, column, whole, send1, recv1, send2, recv2, send3, recv3):
    me, core, deep, plane = place()
    barrier = pltpu.get_barrier_semaphore()
    peers1 = [device_of(plane, lax.rem(deep + d, 8), core) for d in range(1, 8)]
    peers2 = [device_of(lax.rem(plane + d, 16), deep, core) for d in range(1, 16)]
    other = device_of(plane, deep, 1 - core)
    for peer in peers1 + peers2 + [other]:
        pl.semaphore_signal(barrier, inc=1, device_id=(peer,), device_id_type=MESH)

    lane = lax.broadcasted_iota(jnp.int32, (4, 128), 1)
    pivots = pivots_ref[...]
    owners = pivots >> 12
    offsets = pivots & 4095
    mine = owners == me
    key = lane * 4096 + offsets
    first = jnp.min(jnp.where(mine, key, 128 * 4096 - 1), axis=1, keepdims=True) & 4095
    last = jnp.max(jnp.where(mine, key, 0), axis=1, keepdims=True) & 4095
    lanes = lax.broadcasted_iota(jnp.int32, (64, 128), 1)
    lanes2 = lax.broadcasted_iota(jnp.int32, (128, 128), 1)
    packed = jnp.zeros((128, 128), F32)
    for p in range(4):
        halves = []
        for found in (first, last):
            offset = jnp.broadcast_to(found[p:p + 1, 0:1], (64, 128))
            group = offset >> 7
            part = embed_ref[:, 0:128]
            for b in range(1, 32):
                part = jnp.where(group == b, embed_ref[:, 128 * b:128 * b + 128], part)
            halves.append(jnp.sum(jnp.where(lanes == (offset & 127), part, 0.0), axis=1, keepdims=True))
        packed = jnp.where(lanes2 == p, jnp.concatenate(halves, axis=0), packed)
    tile = packed.T[0:4, :]
    own[...] = tile
    column[deep] = tile

    pl.semaphore_wait(barrier, 23)

    copies1 = []
    for d in range(1, 8):
        copy = pltpu.make_async_remote_copy(
            src_ref=own, dst_ref=column.at[deep], send_sem=send1.at[d - 1], recv_sem=recv1.at[deep],
            device_id=(peers1[d - 1],), device_id_type=MESH)
        copy.start()
        copies1.append(copy)

    wanted = []
    sub2 = lax.broadcasted_iota(jnp.int32, (128, 128), 0)
    for p in range(4):
        row = jnp.broadcast_to(owners[p:p + 1, :], (128, 128)).astype(F32)
        col = row.T
        slot = jnp.sum(jnp.where((row == col) & (lanes2 < sub2), 1.0, 0.0), axis=1, keepdims=True)
        owner = col.astype(jnp.int32)
        spot = (owner & 1) * 128 + (owner >> 1)
        wanted.append((spot, slot))

    for start in range(0, 1024, 128):
        one, two = features_of(embed_ref, amp_ref, start)
        features_ref[start:start + 128, 0:128] = one
        features_ref[start:start + 128, 128:256] = two

    for d in range(1, 8):
        source = lax.rem(deep + d, 8)
        pltpu.make_async_remote_copy(
            src_ref=own, dst_ref=column.at[source], send_sem=send1.at[d - 1], recv_sem=recv1.at[source],
            device_id=(peers1[d - 1],), device_id_type=MESH).wait_recv()
    block = core * 16 + plane
    for p in range(4):
        whole[p, block] = jnp.concatenate([column[z][p:p + 1, :] for z in range(8)], axis=0)

    copies2 = []
    for d in range(1, 16):
        copy = pltpu.make_async_remote_copy(
            src_ref=whole.at[:, block], dst_ref=whole.at[:, block], send_sem=send2.at[d - 1], recv_sem=recv2.at[plane],
            device_id=(peers2[d - 1],), device_id_type=MESH)
        copy.start()
        copies2.append(copy)

    def forward(index, of_plane):
        at = core * 16 + of_plane
        copy = pltpu.make_async_remote_copy(
            src_ref=whole.at[:, at], dst_ref=whole.at[:, at], send_sem=send3.at[index], recv_sem=recv3.at[of_plane],
            device_id=(other,), device_id_type=MESH)
        copy.start()
        return copy

    copies3 = [forward(0, plane)]
    for start in range(1024, 4096, 128):
        one, two = features_of(embed_ref, amp_ref, start)
        features_ref[start:start + 128, 0:128] = one
        features_ref[start:start + 128, 128:256] = two

    for d in range(1, 16):
        source = lax.rem(plane + d, 16)
        at = core * 16 + source
        pltpu.make_async_remote_copy(
            src_ref=whole.at[:, at], dst_ref=whole.at[:, at], send_sem=send2.at[d - 1], recv_sem=recv2.at[source],
            device_id=(peers2[d - 1],), device_id_type=MESH).wait_recv()
        copies3.append(forward(d, source))
    for source in range(16):
        at = (1 - core) * 16 + source
        pltpu.make_async_remote_copy(
            src_ref=whole.at[:, at], dst_ref=whole.at[:, at], send_sem=send3.at[0], recv_sem=recv3.at[source],
            device_id=(other,), device_id_type=MESH).wait_recv()

    for p in range(4):
        spot, slot = wanted[p]
        rows = whole[p].reshape(256, 128)
        parts = jnp.concatenate(split_three(rows), axis=1)
        wide = lax.broadcasted_iota(jnp.int32, (128, 256), 1)
        take = jnp.where(wide == jnp.concatenate([spot, spot], axis=1), 1.0, 0.0).astype(BF16)
        got = jnp.dot(take, parts, preferred_element_type=F32)
        got = got[:, 0:128] + (got[:, 128:256] + got[:, 256:384])
        got = jnp.where(slot > 0.5, pltpu.roll(got, 64, 1), got)
        chosen_ref[128 * p:128 * p + 128, :] = jnp.where(lanes2 < 64, got, 0.0)

    for copy in copies1 + copies2 + copies3:
        copy.wait_send()


def gather(pivots, embed, amp):
    return pl.pallas_call(
        gather_kernel,
        out_shape=(jax.ShapeDtypeStruct((4096, 256), BF16), jax.ShapeDtypeStruct((512, 128), F32)),
        in_specs=[pl.BlockSpec(memory_space=pltpu.VMEM)] * 3,
        out_specs=(pl.BlockSpec(memory_space=pltpu.VMEM), pl.BlockSpec(memory_space=pltpu.VMEM)),
        scratch_shapes=[
            pltpu.VMEM((4, 128), F32), pltpu.VMEM((8, 4, 128), F32), pltpu.VMEM((4, 32, 8, 128), F32),
            pltpu.SemaphoreType.DMA((7,)), pltpu.SemaphoreType.DMA((8,)),
            pltpu.SemaphoreType.DMA((15,)), pltpu.SemaphoreType.DMA((16,)),
            pltpu.SemaphoreType.DMA((16,)), pltpu.SemaphoreType.DMA((16,)),
        ],
        compiler_params=pltpu.CompilerParams(collective_id=0, has_side_effects=True, vmem_limit_bytes=32 << 20),
        name="gather_pivots",
    )(pivots, embed, amp)


def product_kernel(features_ref, chosen_ref, amp_ref, factor_ref, residual_ref, sums_ref,
                   matrix, pivots_t, right0, right1, right2, right3):
    step = pl.program_id(0)
    rights = (right0, right1, right2, right3)

    @pl.when(step == 0)
    def _():
        chosen = chosen_ref[...]
        lane = lax.broadcasted_iota(jnp.int32, (512, 128), 1)
        squared = jnp.sum(chosen * chosen, axis=1, keepdims=True) * (LOG2E / 64)
        scaled = chosen * (2 * LOG2E / 64)
        left = jnp.where(lane < 64, chosen, jnp.where(lane == 64, squared, jnp.where(lane == 65, 1.0, 0.0)))
        right = jnp.where(lane < 64, scaled, jnp.where(lane == 64, -1.0, jnp.where(lane == 65, -squared, 0.0)))
        power = lax.dot_general(left, right, (((1,), (1,)), ((), ())), precision=HI, preferred_element_type=F32)
        matrix[...] = jnp.exp2(jnp.minimum(power, 0.0))
        high, low = [v.astype(F32) for v in split_two(scaled)]
        extra = [jnp.full((512, 1), -1.0, F32)] * 3 + [-v.astype(F32) for v in split_three(squared)]
        one = jnp.where(lane < 64, high, pltpu.roll(high, 64, 1))
        two = jnp.where(lane < 64, low, 0.0)
        for index, value in enumerate(extra):
            two = jnp.where(lane == 64 + index, value, two)
        pivots_t[0:128, 0:512] = one.T.astype(BF16)
        pivots_t[128:256, 0:512] = two.T.astype(BF16)
        row = lax.broadcasted_iota(jnp.int32, (256, 128), 0)
        pivots_t[:, 512:640] = jnp.where((row >= 198) & (row < 201), 1.0, 0.0).astype(BF16)

        def store(p, rows):
            for q in range(p + 1):
                high, low = split_two(rows[:, 128 * q:128 * q + 128].T)
                both = jnp.concatenate([high, low], axis=1)
                rights[p][256 * q:256 * q + 128, :] = both
                rights[p][256 * q + 128:256 * q + 256, :] = both

        lower_inverse_512(matrix, store)
        sums_ref[...] = jnp.zeros_like(sums_ref)

    power = jnp.dot(features_ref[...], pivots_t[...], preferred_element_type=F32)
    amp = power[:, 512:640]
    kern = jnp.exp2(jnp.minimum(power[:, 0:512], 0.0))
    high, low = split_two(kern)
    pieces = []
    for q in range(4):
        pieces += [high[:, 128 * q:128 * q + 128], low[:, 128 * q:128 * q + 128]]
    left = jnp.concatenate(pieces, axis=1)
    squares = jnp.zeros((256, 128), F32)
    for p in range(4):
        got = jnp.dot(left[:, :256 * (p + 1)], rights[p][...], preferred_element_type=F32)
        fresh = (got[:, 0:128] + got[:, 128:256]) * amp
        factor_ref[:, 128 * p:128 * p + 128] = fresh
        square = fresh * fresh
        squares += square
        total = square[0:8, :]
        for b in range(1, 32):
            total += square[8 * b:8 * b + 8, :]
        sums_ref[8 * p:8 * p + 8, :] += total
    both = jnp.concatenate(split_two(squares), axis=1)
    spent = lax.dot_general(jnp.ones((8, 256), BF16), both, (((1,), (1,)), ((), ())), preferred_element_type=F32)
    for b in range(2):
        own = amp_ref[pl.ds(2 * step + b, 1), :]
        residual_ref[pl.ds(2 * step + b, 1), :] = own * own - spent[0:1, 128 * b:128 * b + 128]


def product(features, chosen, amp):
    fixed = lambda i: (0, 0)
    return pl.pallas_call(
        product_kernel,
        grid=(16,),
        out_shape=(jax.ShapeDtypeStruct((4096, 512), F32), jax.ShapeDtypeStruct((32, 128), F32),
                   jax.ShapeDtypeStruct((32, 128), F32)),
        in_specs=[pl.BlockSpec((256, 256), lambda i: (i, 0)), pl.BlockSpec((512, 128), fixed),
                  pl.BlockSpec((32, 128), fixed)],
        out_specs=(pl.BlockSpec((256, 512), lambda i: (i, 0)), pl.BlockSpec((32, 128), fixed),
                   pl.BlockSpec((32, 128), fixed)),
        scratch_shapes=[pltpu.VMEM((512, 512), F32), pltpu.VMEM((256, 640), BF16)]
        + [pltpu.VMEM((256 * (p + 1), 256), BF16) for p in range(4)],
        compiler_params=pltpu.CompilerParams(vmem_limit_bytes=48 << 20),
        name="cholesky_product",
    )(features, chosen, amp)


def sums_kernel(points, sums_ref, amp_ref, means_ref, own, land1, middle, land2, send1, recv1, send2, recv2):
    me, core, deep, plane = place()
    line = deep * 2 + core
    barrier = pltpu.get_barrier_semaphore()
    peers1 = [plane * 16 + lax.rem(line + d, 16) for d in range(1, 16)]
    peers2 = [lax.rem(plane + d, 16) * 16 + line for d in range(1, 16)]
    for peer in peers1 + peers2:
        pl.semaphore_signal(barrier, inc=1, device_id=(peer,), device_id_type=MESH)

    lane = lax.broadcasted_iota(jnp.int32, (8, 128), 1)
    total = jnp.sum(amp_ref[...] * amp_ref[...])
    value = jnp.zeros((8, 128), F32)
    for p in range(4):
        total = total - jnp.sum(sums_ref[8 * p:8 * p + 8, :])
        value = jnp.where(lane == p, total, value)
    own[...] = value
    land1[line] = value
    pl.semaphore_wait(barrier, 30)

    def exchange(source, land, at, peers, send, recv):
        copies = []
        for d in range(1, 16):
            copy = pltpu.make_async_remote_copy(
                src_ref=source, dst_ref=land.at[at], send_sem=send.at[d - 1], recv_sem=recv.at[at],
                device_id=(peers[d - 1],), device_id_type=MESH)
            copy.start()
            copies.append(copy)
        for d in range(1, 16):
            origin = lax.rem(at + d, 16)
            pltpu.make_async_remote_copy(
                src_ref=source, dst_ref=land.at[origin], send_sem=send.at[d - 1], recv_sem=recv.at[origin],
                device_id=(peers[d - 1],), device_id_type=MESH).wait_recv()
        return copies, jnp.sum(land[...], axis=0)

    copies1, value = exchange(own, land1, line, peers1, send1, recv1)
    middle[...] = value
    land2[plane] = value
    copies2, value = exchange(middle, land2, plane, peers2, send2, recv2)
    means_ref[...] = value[0:1, 0:4] * (1.0 / points)
    for copy in copies1 + copies2:
        copy.wait_send()


def mean_sums(sums, amp, points):
    return pl.pallas_call(
        functools.partial(sums_kernel, points),
        out_shape=jax.ShapeDtypeStruct((1, 4), F32),
        in_specs=[pl.BlockSpec(memory_space=pltpu.VMEM)] * 2,
        out_specs=pl.BlockSpec(memory_space=pltpu.VMEM),
        scratch_shapes=[
            pltpu.VMEM((8, 128), F32), pltpu.VMEM((16, 8, 128), F32), pltpu.VMEM((8, 128), F32),
            pltpu.VMEM((16, 8, 128), F32),
            pltpu.SemaphoreType.DMA((15,)), pltpu.SemaphoreType.DMA((16,)),
            pltpu.SemaphoreType.DMA((15,)), pltpu.SemaphoreType.DMA((16,)),
        ],
        compiler_params=pltpu.CompilerParams(collective_id=1, has_side_effects=True),
        name="sum_residuals",
    )(sums, amp)


def local(embed, amplitude, pivots):
    amp = amplitude.reshape(32, 128)
    features, chosen = gather(pivots, embed.T, amp)
    factor, residual, sums = product(features, chosen, amp)
    means = mean_sums(sums, amp, 4096 * lax.axis_size("rows"))
    return factor, residual.reshape(4096), means.reshape(4)


def solution(mesh):
    return jax.shard_map(
        local,
        mesh=mesh,
        in_specs=(P("rows", None), P("rows"), P()),
        out_specs=(P("rows", None), P("rows"), P()),
        check_vma=False,
    )
```

time: 689 us -> 71.7 us (0.10)
  blocking collectives: 429 us -> 0 us
  other arithmetic: 129 us -> 0 us
  local copies, waits for them, and re-layouts: 86.6 us -> 5.04 us
  Pallas kernels: 0 us -> 65.5 us
  matrix products: 36.7 us -> 0 us
    all_gather x4 -> x0, blocking collectives: 282 us -> none  [local(): lax.all_gather(packed, 'rows', axis=0, tiled=True)]
    another operation x21 -> x0, other arithmetic: 97.2 us -> none  [the longest x12 51.2 us: lower_inverse(): lower = jnp.linalg.cholesky(0.5 * (block + block.T))]
    unnamed x1 -> x0, blocking collectives: 74.2 us -> none
    psum x1 -> x0, blocking collectives: 73.4 us -> none  [local(): totals = lax.psum(jnp.stack(partial_sums), 'rows')]
    pallas_call x0 -> x3, Pallas kernels: none -> 65.5 us  [the longest x1 27.6 us: product(): pl.pallas_call(product_kernel, grid=(16,), out_shape=(jax.ShapeDtypeStruc...]
    gather x16 -> x0, local copies, waits for them, and re-layouts: 38 us -> none  [the longest x4 14.1 us: local(): chosen_amp = jnp.take(whole_amp, where_from, axis=0)]
    dot_general x26 -> x0, matrix products: 35.5 us -> none  [the longest x8 11.3 us: kernel_block(): jnp.dot(left, right.T, precision=lax.Precision.HIGHEST, preferred_element...]
    concatenate x3 -> x0, local copies, waits for them, and re-layouts: 20.3 us -> none  [local(): source = jnp.concatenate([embed, factor], axis=1)]
where the time goes in v1:
time: 71.7 us; the launch traced here: 71.2 us
  Pallas kernels  65.5 us (91%)
  local copies, waits for them, and re-layouts  5.04 us (7%)
    pallas_call x1, Pallas kernels, product(): pl.pallas_call(product_kernel, grid=(16,), out_shape=(jax.ShapeDtypeStruc...  27.6 us
    pallas_call x1, Pallas kernels, gather(): pl.pallas_call(gather_kernel, out_shape=(jax.ShapeDtypeStruct((4096, 256)...  22.4 us
    pallas_call x1, Pallas kernels, mean_sums(): pl.pallas_call(functools.partial(sums_kernel, points), out_shape=jax.Shap...  15.4 us
    unnamed x11, local copies, waits for them, and re-layouts  5.04 us

profile of v1, /device:TPU:1, one launch (start us, length us, event | category | flops | bytes accessed | tf_op | source)
XLA Modules:
  0.0 71.2 jit_solution(8415286065920231830)
XLA Ops:
  0.6 0.0 copy-start
  0.6 1.2 %copy-done = f32[4096,64]{0,1:T(8,128)S(1)} copy-done((f32[4096,64]{0,1:T(8,128)S(1)}, f32[4096,64]{0,1:T(8,128)}, u32[]{:S(2)}) %copy-start) | copy-done | bytes 1048600
  1.9 0.0 copy-start.1
  1.9 0.7 %copy-done.1 = f32[4096]{0:T(1024)S(1)} copy-done((f32[4096]{0:T(1024)S(1)}, f32[4096]{0:T(1024)}, u32[]{:S(2)}) %copy-start.1) | copy-done | bytes 16408
  2.6 0.0 copy-start.4
  2.6 0.7 copy-done.4
  3.3 22.4 %gather_pivots.1 = (bf16[4096,256]{1,0:T(8,128)(2,1)S(1)}, f32[512,128]{1,0:T(8,128)S(1)}) custom-call(s32[4,128]{1,0:T(4,128)S(1)} %copy-done.4, f32[64,4096]{1,0:T(8,128)S(1)} %bitcast.4, f32[32,128]{1,0:T(8,128)S(1)} %bitcast.6), custom_call_target="tpu_custom_call" | custom-call | tf_op jit(solution)/shard_map/gather_pivots/pallas_call | solution.py:250
  25.7 0.0 copy-start.2
  25.7 0.7 copy-done.2
  26.4 27.6 %cholesky_product.1 = (f32[4096,512]{1,0:T(8,128)}, f32[32,128]{1,0:T(8,128)}, f32[32,128]{1,0:T(8,128)S(1)}) custom-call(bf16[4096,256]{1,0:T(8,128)(2,1)S(1)} %get-tuple-element.8.features_ref, f32[512,128]{1,0:T(8,128)S(1)} %get-tuple-element.9.chosen_ref, f32[32,128]{1,0:T(8,128)S(1)} %bitcast.7), custom_call_target="tpu_custom_call" | custom-call | tf_op jit(solution)/shard_map/cholesky_product/pallas_call | solution.py:330
  54.1 0.0 copy-start.3
  54.1 0.6 copy-done.3
  54.7 15.4 %sum_residuals.1 = f32[1,4]{1,0:T(1,128)} custom-call(f32[32,128]{1,0:T(8,128)} %copy-done.3, f32[32,128]{1,0:T(8,128)} %bitcast.5), custom_call_target="tpu_custom_call" | custom-call | tf_op jit(solution)/shard_map/sum_residuals/pallas_call | solution.py:390
  70.1 1.1 %copy.7 = f32[4]{0:T(128)} copy(f32[4]{0:T(128)} %bitcast.8) | data formatting | bytes 32
Async XLA Ops:
  0.6 1.2 %copy-start = (f32[4096,64]{0,1:T(8,128)S(1)}, f32[4096,64]{0,1:T(8,128)}, u32[]{:S(2)}) copy-start(f32[4096,64]{0,1:T(8,128)} %param.3) | copy-start | bytes 3145732
  1.9 0.7 %copy-start.1 = (f32[4096]{0:T(1024)S(1)}, f32[4096]{0:T(1024)}, u32[]{:S(2)}) copy-start(f32[4096]{0:T(1024)} %param.4) | copy-start | bytes 49156
  2.6 0.7 copy-start.4
  25.7 0.7 %copy-start.2 = (f32[4096]{0:T(1024)S(1)}, f32[4096]{0:T(1024)}, u32[]{:S(2)}) copy-start(f32[4096]{0:T(1024)} %param.4) | copy-start | bytes 49156
  54.1 0.6 copy-start.3

commit v2 on v1

--- a/solution.py
+++ b/solution.py
@@ -6,26 +6,41 @@
 from jax.experimental import pallas as pl
 from jax.experimental.pallas import tpu as pltpu
 from jax.sharding import PartitionSpec as P
+
 HI = lax.Precision.HIGHEST
 F32 = jnp.float32
 
+LOG2E = 1.4426950408889634
+MESH = pl.DeviceIdType.MESH
+BF16 = jnp.bfloat16
+
+
 def spread_row(block, row):
-    return jnp.broadcast_to(block[row:row+1, :], (8, 128))
+    return jnp.broadcast_to(block[row:row + 1, :], (8, 128))
+
 
 def spread_col(block, col):
-    return jnp.broadcast_to(block[:, col:col+1], (8, 128))
-
-def eliminate(blocks, lookahead=True):
+    return jnp.broadcast_to(block[:, col:col + 1], (8, 128))
+
+
+def tree(terms):
+    while len(terms) > 1:
+        terms = [a + b for a, b in zip(terms[::2], terms[1::2])] + ([terms[-1]] if len(terms) % 2 else [])
+    return terms[0]
+
+
+def eliminate_rows(blocks, base, work, step):
     lane = lax.broadcasted_iota(jnp.int32, (8, 128), 1)
     sub = lax.broadcasted_iota(jnp.int32, (8, 128), 0)
-    n = len(blocks)
+    count = len(blocks)
     blocks = list(blocks)
-    diag = [spread_col(blocks[0], k) for k in range(8)]
-    for j in range(n):
-        inside = (lane >= 8 * j) & (lane < 8 * j + 8)
-        below = {b: [spread_col(blocks[b], 8 * j + k) for k in range(8)] for b in range(j + 1, n)}
-        nxt = [spread_col(blocks[j + 1], 8 * (j + 1) + k) for k in range(8)] if j + 1 < n else None
-        rest = jnp.where(inside, jnp.where(lane - 8 * j == sub, 1.0, 0.0), blocks[j])
+    diag = [spread_col(blocks[0], base + k) for k in range(8)]
+    for j in range(count):
+        at = base + 8 * j
+        inside = (lane >= at) & (lane < at + 8)
+        below = {b: [spread_col(blocks[b], at + k) for k in range(8)] for b in range(j + 1, count)}
+        following = [spread_col(blocks[j + 1], at + 8 + k) for k in range(8)] if j + 1 < count else None
+        rest = jnp.where(inside, jnp.where(lane - at == sub, 1.0, 0.0), blocks[j])
         rows = []
         for k in range(8):
             scale = lax.rsqrt(spread_row(diag[k], k))
@@ -41,49 +56,37 @@
                 diag[m] = diag[m] - low * factor
                 for b in below:
                     below[b][m] = below[b][m] - below[b][k] * factor
+            step()
         out = rows[0]
         for k in range(1, 8):
             out = jnp.where(sub == k, rows[k], out)
         blocks[j] = out
-        if j + 1 < n:
-            w = below[j + 1]
-            for k in range(8):
-                t = [w[l] * spread_row(w[l], k) for l in range(8)]
-                t = ((t[0] + t[1]) + (t[2] + t[3])) + ((t[4] + t[5]) + (t[6] + t[7]))
-                nxt[k] = nxt[k] - t
-            diag = nxt
+        if j + 1 < count:
+            first = below[j + 1]
+            diag = [following[k] - tree([first[m] * spread_row(first[m], k) for m in range(8)]) for k in range(8)]
         for b in below:
-            t = [below[b][l] * rows[l] for l in range(8)]
-            t = ((t[0] + t[1]) + (t[2] + t[3])) + ((t[4] + t[5]) + (t[6] + t[7]))
-            blocks[b] = jnp.where(inside, 0.0, blocks[b]) - t
+            blocks[b] = jnp.where(inside, 0.0, blocks[b]) - tree([below[b][k] * rows[k] for k in range(8)])
+        work(at // 8)
     return blocks
 
-def lower_inverse_512(a_ref, store):
-    lane = lax.broadcasted_iota(jnp.int32, (128, 128), 1)
-    sub = lax.broadcasted_iota(jnp.int32, (128, 128), 0)
-    size = a_ref.shape[0]
-    panels = size // 128
-    for p in range(panels):
-        lo = 128 * p
-        got = eliminate([a_ref[lo + 8 * b: lo + 8 * b + 8, lo:lo + 128] for b in range(16)])
-        inv = jnp.where(lane <= sub, jnp.concatenate(got, axis=0), 0.0)
-        right = None
-        if p + 1 < panels:
-            right = jnp.dot(inv, a_ref[lo:lo + 128, lo + 128:], precision=HI, preferred_element_type=F32)
-            a_ref[lo + 128:, lo + 128:] -= lax.dot_general(right, right, (((0,), (0,)), ((), ())), precision=HI, preferred_element_type=F32)
-        left = inv
-        if p:
-            left = jnp.concatenate([jnp.dot(inv, a_ref[lo:lo + 128, :lo], precision=HI, preferred_element_type=F32), inv], axis=1)
-        store(p, left)
-        if p + 1 < panels:
-            upd = lax.dot_general(right, left, (((0,), (0,)), ((), ())), precision=HI, preferred_element_type=F32)
-            if p:
-                a_ref[lo + 128:, :lo] -= upd[:, :lo]
-            a_ref[lo + 128:, lo:lo + 128] = -upd[:, lo:]
-
-LOG2E = 1.4426950408889634
-MESH = pl.DeviceIdType.MESH
-BF16 = jnp.bfloat16
+
+def eliminate(blocks, work, step, width=64):
+    lane = lax.broadcasted_iota(jnp.int32, (8, 128), 1)
+    blocks = list(blocks)
+    group = width // 8
+    for base in range(0, 128, width):
+        first = base // 8
+        blocks[first:first + group] = eliminate_rows(blocks[first:first + group], base, work, step)
+        if base + width < 128:
+            rows = jnp.concatenate(blocks[first:first + group], axis=0)
+            row = lax.broadcasted_iota(jnp.int32, (width, 128), 0) + base
+            col = lax.broadcasted_iota(jnp.int32, (width, 128), 1)
+            lower = jnp.where((col > row) & (col < base + width), 0.0, rows)
+            change = lax.dot_general(rows, lower, (((0,), (0,)), ((), ())), precision=HI, preferred_element_type=F32)
+            inside = (lane >= base) & (lane < base + width)
+            for b in range(first + group, 16):
+                blocks[b] = jnp.where(inside, 0.0, blocks[b]) - change[8 * b:8 * b + 8, :]
+    return blocks
 
 
 def split_two(value):
@@ -96,6 +99,151 @@
     left = value - high.astype(F32)
     middle = left.astype(BF16)
     return high, middle, (left - middle.astype(F32)).astype(BF16)
+
+
+def both_parts(value):
+    both = jnp.concatenate(split_two(value), axis=1)
+    return jnp.concatenate([both, both], axis=0)
+
+
+def halves(value):
+    return value[:, 0:128] + value[:, 128:256]
+
+
+def prepare(chosen, matrix, pivots_t):
+    lane = lax.broadcasted_iota(jnp.int32, (512, 128), 1)
+    squared = jnp.sum(chosen * chosen, axis=1, keepdims=True) * (LOG2E / 64)
+    scaled = chosen * (2 * LOG2E / 64)
+    left = jnp.where(lane < 64, chosen, jnp.where(lane == 64, squared, jnp.where(lane == 65, 1.0, 0.0)))
+    right = jnp.where(lane < 64, scaled, jnp.where(lane == 64, -1.0, jnp.where(lane == 65, -squared, 0.0)))
+    power = lax.dot_general(left, right, (((1,), (1,)), ((), ())), precision=HI, preferred_element_type=F32)
+    matrix[...] = jnp.exp2(jnp.minimum(power, 0.0))
+    high, low = [v.astype(F32) for v in split_two(scaled)]
+    extra = [jnp.full((512, 1), -1.0, F32)] * 3 + [-v.astype(F32) for v in split_three(squared)]
+    one = jnp.where(lane < 64, high, pltpu.roll(high, 64, 1))
+    two = jnp.where(lane < 64, low, 0.0)
+    for index, value in enumerate(extra):
+        two = jnp.where(lane == 64 + index, value, two)
+    pivots_t[0:128, 0:512] = one.T.astype(BF16)
+    pivots_t[128:256, 0:512] = two.T.astype(BF16)
+    row = lax.broadcasted_iota(jnp.int32, (256, 128), 0)
+    pivots_t[:, 512:640] = jnp.where((row >= 198) & (row < 201), 1.0, 0.0).astype(BF16)
+
+
+CHUNK = 256
+CHUNKS = 4096 // CHUNK
+PIECE = 32
+PER_STEP = 2
+
+
+def factorise(features_ref, amp_ref, matrix, pivots_t, kern, cross, done, wide_amp, squares, inverse_t, upper,
+              raw_first, raw_near, raw_far, staged, residual_ref, sent):
+    sums = [[] for _ in range(4)]
+    pending = []
+
+    def step(count=PER_STEP):
+        for _ in range(min(count, len(pending))):
+            pending.pop(0)()
+
+    def pieces(j):
+        return [(slice(CHUNK * j + r, CHUNK * j + r + PIECE), slice(r, r + PIECE)) for r in range(0, CHUNK, PIECE)]
+
+    def start_first(j):
+        raw_first[j % 2] = jnp.dot(
+            features_ref[CHUNK * j:CHUNK * j + CHUNK, :], pivots_t[...], preferred_element_type=F32)
+
+    def end_first(j, at, part):
+        wide_amp[at, :] = raw_first[j % 2, part, 512:640]
+        near = jnp.exp2(jnp.minimum(raw_first[j % 2, part, 0:512], 0.0))
+        cross[at, :] = jnp.concatenate(split_two(near[:, 0:128]), axis=1)
+        kern[at, :] = near[:, 128:512]
+
+    def start_near(p, j):
+        raw_near[j % 2] = jnp.dot(
+            cross[CHUNK * j:CHUNK * j + CHUNK, :], inverse_t[p], preferred_element_type=F32)
+
+    def end_near(p, j, at, part):
+        got = halves(raw_near[j % 2, part, :])
+        fresh = got * wide_amp[at, :]
+        staged[p, at, :] = fresh
+        square = fresh * fresh
+        sums[p].append(tree([square[8 * b:8 * b + 8, :] for b in range(PIECE // 8)]))
+        if p < 3:
+            squares[at, :] = square if p == 0 else squares[at, :] + square
+            done[at, 256 * p:256 * p + 256] = jnp.concatenate(split_two(got), axis=1)
+        else:
+            squares[at, :] = squares[at, :] + square
+
+    def start_far(p, j):
+        raw_far[j % 2] = jnp.dot(
+            done[CHUNK * j:CHUNK * j + CHUNK, 0:256 * (p + 1)], upper[p + 1][...], preferred_element_type=F32)
+
+    def end_far(p, j, at, part):
+        rest = kern[at, 128 * p:128 * p + 128] - halves(raw_far[j % 2, part, :])
+        cross[at, :] = jnp.concatenate(split_two(rest), axis=1)
+
+    def residual_of(j):
+        both = jnp.concatenate(split_two(squares[CHUNK * j:CHUNK * j + CHUNK, :]), axis=1)
+        spent = lax.dot_general(jnp.ones((8, 256), BF16), both, (((1,), (1,)), ((), ())), preferred_element_type=F32)
+        for b in range(CHUNK // 128):
+            row = j * (CHUNK // 128) + b
+            own = amp_ref[row:row + 1, :]
+            residual_ref[row:row + 1, :] = own * own - spent[0:1, 128 * b:128 * b + 128]
+
+    def schedule(t):
+        if 0 <= t < 16:
+            start_first(t)
+        if 1 <= t < 17:
+            pending.extend(functools.partial(end_first, t - 1, *piece) for piece in pieces(t - 1))
+        if 16 <= t < 80:
+            start_near(t // 16 - 1, t % 16)
+        if 18 <= t < 66:
+            p, j = (t - 2) // 16 - 1, (t - 2) % 16
+            pending.extend(functools.partial(end_far, p, j, *piece) for piece in pieces(j))
+        if 17 <= t < 81:
+            p, j = (t - 1) // 16 - 1, (t - 1) % 16
+            pending.extend(functools.partial(end_near, p, j, *piece) for piece in pieces(j))
+            pending.append(functools.partial(sent, p, j))
+            if p < 3:
+                pending.append(functools.partial(start_far, p, j))
+        if 66 <= t < 82:
+            pending.append(functools.partial(residual_of, t - 66))
+
+    lane = lax.broadcasted_iota(jnp.int32, (128, 128), 1)
+    sub = lax.broadcasted_iota(jnp.int32, (128, 128), 0)
+    for p in range(4):
+        lo = 128 * p
+
+        def work(j):
+            step(len(pending))
+            if j < 15:
+                schedule(16 * p + j + 1)
+
+        schedule(16 * p)
+        got = eliminate([matrix[lo + 8 * b:lo + 8 * b + 8, lo:lo + 128] for b in range(16)], work, step)
+        inverse = jnp.where(lane <= sub, jnp.concatenate(got, axis=0), 0.0)
+        inverse_t[p] = both_parts(inverse.T)
+        if p < 3:
+            right = jnp.dot(inverse, matrix[lo:lo + 128, lo + 128:], precision=HI, preferred_element_type=F32)
+            for q in range(p + 1, 4):
+                part = right[:, 128 * (q - p - 1):128 * (q - p)]
+                matrix[128 * q:128 * q + 128, 128 * q:] -= lax.dot_general(
+                    part, right[:, 128 * (q - p - 1):], (((0,), (0,)), ((), ())), precision=HI,
+                    preferred_element_type=F32)
+                upper[q][256 * p:256 * p + 256, :] = both_parts(part)
+    for t in range(64, 82):
+        schedule(t)
+        step(len(pending))
+    return [tree(parts) for parts in sums]
+
+
+SCRATCH = [
+    pltpu.VMEM((512, 512), F32), pltpu.VMEM((256, 640), BF16), pltpu.VMEM((4096, 384), F32),
+    pltpu.VMEM((4096, 256), BF16), pltpu.VMEM((4096, 768), BF16), pltpu.VMEM((4096, 128), F32),
+    pltpu.VMEM((4096, 128), F32), pltpu.VMEM((4, 256, 256), BF16),
+    pltpu.VMEM((256, 256), BF16), pltpu.VMEM((512, 256), BF16), pltpu.VMEM((768, 256), BF16),
+    pltpu.VMEM((2, CHUNK, 640), F32), pltpu.VMEM((2, CHUNK, 256), F32), pltpu.VMEM((2, CHUNK, 256), F32),
+]
 
 
 def place():
@@ -127,9 +275,16 @@
     return one, two
 
 
-def gather_kernel(pivots_ref, embed_ref, amp_ref, features_ref, chosen_ref,
-                  own, column, whole, send1, recv1, send2, recv2, send3, recv3):
+def gather_kernel(pivots_hbm, embed_hbm, amp_hbm, features_ref, chosen_ref,
+                  pivots_ref, embed_ref, amp_ref, loaded, own, column, whole, send1, recv1, send2, recv2, send3, recv3):
     me, core, deep, plane = place()
+    loads = [
+        pltpu.make_async_copy(pivots_hbm, pivots_ref, loaded.at[0]),
+        pltpu.make_async_copy(embed_hbm, embed_ref, loaded.at[1]),
+        pltpu.make_async_copy(amp_hbm, amp_ref, loaded.at[2]),
+    ]
+    for load in loads:
+        load.start()
     barrier = pltpu.get_barrier_semaphore()
     peers1 = [device_of(plane, lax.rem(deep + d, 8), core) for d in range(1, 8)]
     peers2 = [device_of(lax.rem(plane + d, 16), deep, core) for d in range(1, 16)]
@@ -137,6 +292,8 @@
     for peer in peers1 + peers2 + [other]:
         pl.semaphore_signal(barrier, inc=1, device_id=(peer,), device_id_type=MESH)
 
+    for load in loads:
+        load.wait()
     lane = lax.broadcasted_iota(jnp.int32, (4, 128), 1)
     pivots = pivots_ref[...]
     owners = pivots >> 12
@@ -250,9 +407,11 @@
     return pl.pallas_call(
         gather_kernel,
         out_shape=(jax.ShapeDtypeStruct((4096, 256), BF16), jax.ShapeDtypeStruct((512, 128), F32)),
-        in_specs=[pl.BlockSpec(memory_space=pltpu.VMEM)] * 3,
+        in_specs=[pl.BlockSpec(memory_space=pltpu.HBM)] * 3,
         out_specs=(pl.BlockSpec(memory_space=pltpu.VMEM), pl.BlockSpec(memory_space=pltpu.VMEM)),
         scratch_shapes=[
+            pltpu.VMEM((4, 128), jnp.int32), pltpu.VMEM((64, 4096), F32), pltpu.VMEM((32, 128), F32),
+            pltpu.SemaphoreType.DMA((3,)),
             pltpu.VMEM((4, 128), F32), pltpu.VMEM((8, 4, 128), F32), pltpu.VMEM((4, 32, 8, 128), F32),
             pltpu.SemaphoreType.DMA((7,)), pltpu.SemaphoreType.DMA((8,)),
             pltpu.SemaphoreType.DMA((15,)), pltpu.SemaphoreType.DMA((16,)),
@@ -264,81 +423,37 @@
 
 
 def product_kernel(features_ref, chosen_ref, amp_ref, factor_ref, residual_ref, sums_ref,
-                   matrix, pivots_t, right0, right1, right2, right3):
-    step = pl.program_id(0)
-    rights = (right0, right1, right2, right3)
-
-    @pl.when(step == 0)
-    def _():
-        chosen = chosen_ref[...]
-        lane = lax.broadcasted_iota(jnp.int32, (512, 128), 1)
-        squared = jnp.sum(chosen * chosen, axis=1, keepdims=True) * (LOG2E / 64)
-        scaled = chosen * (2 * LOG2E / 64)
-        left = jnp.where(lane < 64, chosen, jnp.where(lane == 64, squared, jnp.where(lane == 65, 1.0, 0.0)))
-        right = jnp.where(lane < 64, scaled, jnp.where(lane == 64, -1.0, jnp.where(lane == 65, -squared, 0.0)))
-        power = lax.dot_general(left, right, (((1,), (1,)), ((), ())), precision=HI, preferred_element_type=F32)
-        matrix[...] = jnp.exp2(jnp.minimum(power, 0.0))
-        high, low = [v.astype(F32) for v in split_two(scaled)]
-        extra = [jnp.full((512, 1), -1.0, F32)] * 3 + [-v.astype(F32) for v in split_three(squared)]
-        one = jnp.where(lane < 64, high, pltpu.roll(high, 64, 1))
-        two = jnp.where(lane < 64, low, 0.0)
-        for index, value in enumerate(extra):
-            two = jnp.where(lane == 64 + index, value, two)
-        pivots_t[0:128, 0:512] = one.T.astype(BF16)
-        pivots_t[128:256, 0:512] = two.T.astype(BF16)
-        row = lax.broadcasted_iota(jnp.int32, (256, 128), 0)
-        pivots_t[:, 512:640] = jnp.where((row >= 198) & (row < 201), 1.0, 0.0).astype(BF16)
-
-        def store(p, rows):
-            for q in range(p + 1):
-                high, low = split_two(rows[:, 128 * q:128 * q + 128].T)
-                both = jnp.concatenate([high, low], axis=1)
-                rights[p][256 * q:256 * q + 128, :] = both
-                rights[p][256 * q + 128:256 * q + 256, :] = both
-
-        lower_inverse_512(matrix, store)
-        sums_ref[...] = jnp.zeros_like(sums_ref)
-
-    power = jnp.dot(features_ref[...], pivots_t[...], preferred_element_type=F32)
-    amp = power[:, 512:640]
-    kern = jnp.exp2(jnp.minimum(power[:, 0:512], 0.0))
-    high, low = split_two(kern)
-    pieces = []
-    for q in range(4):
-        pieces += [high[:, 128 * q:128 * q + 128], low[:, 128 * q:128 * q + 128]]
-    left = jnp.concatenate(pieces, axis=1)
-    squares = jnp.zeros((256, 128), F32)
-    for p in range(4):
-        got = jnp.dot(left[:, :256 * (p + 1)], rights[p][...], preferred_element_type=F32)
-        fresh = (got[:, 0:128] + got[:, 128:256]) * amp
-        factor_ref[:, 128 * p:128 * p + 128] = fresh
-        square = fresh * fresh
-        squares += square
-        total = square[0:8, :]
-        for b in range(1, 32):
-            total += square[8 * b:8 * b + 8, :]
-        sums_ref[8 * p:8 * p + 8, :] += total
-    both = jnp.concatenate(split_two(squares), axis=1)
-    spent = lax.dot_general(jnp.ones((8, 256), BF16), both, (((1,), (1,)), ((), ())), preferred_element_type=F32)
-    for b in range(2):
-        own = amp_ref[pl.ds(2 * step + b, 1), :]
-        residual_ref[pl.ds(2 * step + b, 1), :] = own * own - spent[0:1, 128 * b:128 * b + 128]
+                   matrix, pivots_t, kern, cross, done, wide_amp, squares, inverse_t, upper1, upper2, upper3,
+                   raw_first, raw_near, raw_far, staged, sems):
+    prepare(chosen_ref[...], matrix, pivots_t)
+    copies = []
+
+    def sent(p, j):
+        if j % 4 == 3:
+            rows = pl.ds(CHUNK * (j - 3), 4 * CHUNK)
+            copy = pltpu.make_async_copy(
+                staged.at[p, rows], factor_ref.at[rows, pl.ds(128 * p, 128)], sems.at[4 * p + j // 4])
+            copy.start()
+            copies.append(copy)
+
+    sums = factorise(features_ref, amp_ref, matrix, pivots_t, kern, cross, done, wide_amp, squares, inverse_t,
+                     (None, upper1, upper2, upper3), raw_first, raw_near, raw_far, staged, residual_ref, sent)
+    for p in range(4):
+        sums_ref[8 * p:8 * p + 8, :] = sums[p]
+    for copy in copies:
+        copy.wait()
 
 
 def product(features, chosen, amp):
-    fixed = lambda i: (0, 0)
     return pl.pallas_call(
         product_kernel,
-        grid=(16,),
         out_shape=(jax.ShapeDtypeStruct((4096, 512), F32), jax.ShapeDtypeStruct((32, 128), F32),
                    jax.ShapeDtypeStruct((32, 128), F32)),
-        in_specs=[pl.BlockSpec((256, 256), lambda i: (i, 0)), pl.BlockSpec((512, 128), fixed),
-                  pl.BlockSpec((32, 128), fixed)],
-        out_specs=(pl.BlockSpec((256, 512), lambda i: (i, 0)), pl.BlockSpec((32, 128), fixed),
-                   pl.BlockSpec((32, 128), fixed)),
-        scratch_shapes=[pltpu.VMEM((512, 512), F32), pltpu.VMEM((256, 640), BF16)]
-        + [pltpu.VMEM((256 * (p + 1), 256), BF16) for p in range(4)],
-        compiler_params=pltpu.CompilerParams(vmem_limit_bytes=48 << 20),
+        in_specs=[pl.BlockSpec(memory_space=pltpu.VMEM)] * 3,
+        out_specs=(pl.BlockSpec(memory_space=pltpu.HBM), pl.BlockSpec(memory_space=pltpu.VMEM),
+                   pl.BlockSpec(memory_space=pltpu.VMEM)),
+        scratch_shapes=SCRATCH + [pltpu.VMEM((4, 4096, 128), F32), pltpu.SemaphoreType.DMA((16,))],
+        compiler_params=pltpu.CompilerParams(vmem_limit_bytes=50 << 20),
         name="cholesky_product",
     )(features, chosen, amp)
 

time: 71.7 us -> 62.1 us (0.87)
  Pallas kernels: 65.5 us -> 55.9 us
    pallas_call x1, Pallas kernels: 27.6 us -> 17.8 us  [product(): pl.pallas_call(product_kernel, out_shape=(jax.ShapeDtypeStruct((4096, 512...]
where the time goes in v2:
time: 62.1 us; the launch traced here: 61.6 us
  Pallas kernels  55.9 us (90%)
  local copies, waits for them, and re-layouts  5.03 us (8%)
  between operations  0.68 us (1%)
    pallas_call x1, Pallas kernels, gather(): pl.pallas_call(gather_kernel, out_shape=(jax.ShapeDtypeStruct((4096, 256)...  22.7 us
    pallas_call x1, Pallas kernels, product(): pl.pallas_call(product_kernel, out_shape=(jax.ShapeDtypeStruct((4096, 512...  17.8 us
    pallas_call x1, Pallas kernels, mean_sums(): pl.pallas_call(functools.partial(sums_kernel, points), out_shape=jax.Shap...  15.4 us
    unnamed x11, local copies, waits for them, and re-layouts  5.03 us

profile of v2, /device:TPU:1, one launch (start us, length us, event | category | flops | bytes accessed | tf_op | source)
XLA Modules:
  0.0 61.6 jit_solution(644813722748959415)
XLA Ops:
  0.6 0.0 copy-start
  0.6 1.2 %copy-done = f32[4096,64]{0,1:T(8,128)S(1)} copy-done((f32[4096,64]{0,1:T(8,128)S(1)}, f32[4096,64]{0,1:T(8,128)}, u32[]{:S(2)}) %copy-start) | copy-done | bytes 1048600
  1.9 0.0 copy-start.1
  1.9 0.7 %copy-done.1 = f32[4096]{0:T(1024)S(1)} copy-done((f32[4096]{0:T(1024)S(1)}, f32[4096]{0:T(1024)}, u32[]{:S(2)}) %copy-start.1) | copy-done | bytes 16408
  2.6 0.0 copy-start.4
  2.6 0.7 %copy-done.4 = s32[4,128]{1,0:T(4,128)S(1)} copy-done((s32[4,128]{1,0:T(4,128)S(1)}, s32[4,128]{1,0:T(4,128)}, u32[]{:S(2)}) %copy-start.4) | copy-done | bytes 2072
  3.3 22.7 %gather_pivots.1 = (bf16[4096,256]{1,0:T(8,128)(2,1)S(1)}, f32[512,128]{1,0:T(8,128)S(1)}) custom-call(s32[4,128]{1,0:T(4,128)S(1)} %copy-done.4, f32[64,4096]{1,0:T(8,128)S(1)} %bitcast.4, f32[32,128]{1,0:T(8,128)S(1)} %bitcast.6), custom_call_target="tpu_custom_call" | custom-call | tf_op jit(solution)/shard_map/gather_pivots/pallas_call | solution.py:407
  26.0 0.0 copy-start.2
  26.0 0.7 %copy-done.2 = f32[4096]{0:T(1024)S(1)} copy-done((f32[4096]{0:T(1024)S(1)}, f32[4096]{0:T(1024)}, u32[]{:S(2)}) %copy-start.2) | copy-done | bytes 16408
  26.7 17.8 %cholesky_product.1 = (f32[4096,512]{1,0:T(8,128)}, f32[32,128]{1,0:T(8,128)}, f32[32,128]{1,0:T(8,128)S(1)}) custom-call(bf16[4096,256]{1,0:T(8,128)(2,1)S(1)} %get-tuple-element.8.features_ref, f32[512,128]{1,0:T(8,128)S(1)} %get-tuple-element.9.chosen_ref, f32[32,128]{1,0:T(8,128)S(1)} %bitcast.7), custom_call_target="tpu_custom_call" | custom-call | tf_op jit(solution)/shard_map/cholesky_product/pallas_call | solution.py:448
  44.5 0.0 copy-start.3
  44.5 0.6 copy-done.3
  45.1 15.4 %sum_residuals.1 = f32[1,4]{1,0:T(1,128)} custom-call(f32[32,128]{1,0:T(8,128)} %copy-done.3, f32[32,128]{1,0:T(8,128)} %bitcast.5), custom_call_target="tpu_custom_call" | custom-call | tf_op jit(solution)/shard_map/sum_residuals/pallas_call | solution.py:505
  60.5 1.1 %copy.7 = f32[4]{0:T(128)} copy(f32[4]{0:T(128)} %bitcast.8) | data formatting | bytes 32
Async XLA Ops:
  0.6 1.2 %copy-start = (f32[4096,64]{0,1:T(8,128)S(1)}, f32[4096,64]{0,1:T(8,128)}, u32[]{:S(2)}) copy-start(f32[4096,64]{0,1:T(8,128)} %param.3) | copy-start | bytes 3145732
  1.9 0.7 %copy-start.1 = (f32[4096]{0:T(1024)S(1)}, f32[4096]{0:T(1024)}, u32[]{:S(2)}) copy-start(f32[4096]{0:T(1024)} %param.4) | copy-start | bytes 49156
  2.6 0.7 %copy-start.4 = (s32[4,128]{1,0:T(4,128)S(1)}, s32[4,128]{1,0:T(4,128)}, u32[]{:S(2)}) copy-start(s32[4,128]{1,0:T(4,128)} %pivots_hbm.1) | copy-start | bytes 6148
  26.0 0.7 %copy-start.2 = (f32[4096]{0:T(1024)S(1)}, f32[4096]{0:T(1024)}, u32[]{:S(2)}) copy-start(f32[4096]{0:T(1024)} %param.4) | copy-start | bytes 49156
  44.5 0.6 copy-start.3

commit v3 on v2

--- a/solution.py
+++ b/solution.py
@@ -120,6 +120,7 @@
     matrix[...] = jnp.exp2(jnp.minimum(power, 0.0))
     high, low = [v.astype(F32) for v in split_two(scaled)]
     extra = [jnp.full((512, 1), -1.0, F32)] * 3 + [-v.astype(F32) for v in split_three(squared)]
+    extra += [jnp.full((512, 1), 1.0, F32)] * 3
     one = jnp.where(lane < 64, high, pltpu.roll(high, 64, 1))
     two = jnp.where(lane < 64, low, 0.0)
     for index, value in enumerate(extra):
@@ -136,8 +137,8 @@
 PER_STEP = 2
 
 
-def factorise(features_ref, amp_ref, matrix, pivots_t, kern, cross, done, wide_amp, squares, inverse_t, upper,
-              raw_first, raw_near, raw_far, staged, residual_ref, sent):
+def factorise(features_ref, amp_ref, matrix, pivots_t, kern, cross, done, squares, inverse_t, upper,
+              raw_first, raw_near, raw_far, factor_ref, residual_ref):
     sums = [[] for _ in range(4)]
     pending = []
 
@@ -153,10 +154,10 @@
             features_ref[CHUNK * j:CHUNK * j + CHUNK, :], pivots_t[...], preferred_element_type=F32)
 
     def end_first(j, at, part):
-        wide_amp[at, :] = raw_first[j % 2, part, 512:640]
-        near = jnp.exp2(jnp.minimum(raw_first[j % 2, part, 0:512], 0.0))
-        cross[at, :] = jnp.concatenate(split_two(near[:, 0:128]), axis=1)
-        kern[at, :] = near[:, 128:512]
+        top = raw_first[j % 2, part, 512:640]
+        near = [jnp.exp2(jnp.minimum(raw_first[j % 2, part, 128 * q:128 * q + 128], top)) for q in range(4)]
+        cross[at, :] = jnp.concatenate(split_two(near[0]), axis=1)
+        kern[at, :] = jnp.concatenate(near[1:], axis=1)
 
     def start_near(p, j):
         raw_near[j % 2] = jnp.dot(
@@ -164,9 +165,8 @@
 
     def end_near(p, j, at, part):
         got = halves(raw_near[j % 2, part, :])
-        fresh = got * wide_amp[at, :]
-        staged[p, at, :] = fresh
-        square = fresh * fresh
+        factor_ref[at, 128 * p:128 * p + 128] = got
+        square = got * got
         sums[p].append(tree([square[8 * b:8 * b + 8, :] for b in range(PIECE // 8)]))
         if p < 3:
             squares[at, :] = square if p == 0 else squares[at, :] + square
@@ -203,7 +203,6 @@
         if 17 <= t < 81:
             p, j = (t - 1) // 16 - 1, (t - 1) % 16
             pending.extend(functools.partial(end_near, p, j, *piece) for piece in pieces(j))
-            pending.append(functools.partial(sent, p, j))
             if p < 3:
                 pending.append(functools.partial(start_far, p, j))
         if 66 <= t < 82:
@@ -240,7 +239,7 @@
 SCRATCH = [
     pltpu.VMEM((512, 512), F32), pltpu.VMEM((256, 640), BF16), pltpu.VMEM((4096, 384), F32),
     pltpu.VMEM((4096, 256), BF16), pltpu.VMEM((4096, 768), BF16), pltpu.VMEM((4096, 128), F32),
-    pltpu.VMEM((4096, 128), F32), pltpu.VMEM((4, 256, 256), BF16),
+    pltpu.VMEM((4, 256, 256), BF16),
     pltpu.VMEM((256, 256), BF16), pltpu.VMEM((512, 256), BF16), pltpu.VMEM((768, 256), BF16),
     pltpu.VMEM((2, CHUNK, 640), F32), pltpu.VMEM((2, CHUNK, 256), F32), pltpu.VMEM((2, CHUNK, 256), F32),
 ]
@@ -260,7 +259,7 @@
 
 def features_of(embed_ref, amp_ref, first):
     part = embed_ref[:, first:first + 128]
-    amp = amp_ref[first // 128:first // 128 + 1, :]
+    amp = jnp.log2(amp_ref[first // 128:first // 128 + 1, :])
     squared = jnp.sum(part * part, axis=0, keepdims=True) * (LOG2E / 64)
     high, low = split_two(part)
     high, low = high.astype(F32), low.astype(F32)
@@ -275,8 +274,12 @@
     return one, two
 
 
-def gather_kernel(pivots_hbm, embed_hbm, amp_hbm, features_ref, chosen_ref,
-                  pivots_ref, embed_ref, amp_ref, loaded, own, column, whole, send1, recv1, send2, recv2, send3, recv3):
+def whole_kernel(points, pivots_hbm, embed_hbm, amp_hbm, factor_ref, residual_ref, means_ref,
+                 pivots_ref, embed_ref, amp_ref, loaded, features_ref, chosen_ref,
+                 own, column, whole, send1, recv1, send2, recv2, send3, recv3,
+                 mine1, mine2, land2, mine3, land3, total_sems,
+                 matrix, pivots_t, kern, cross, done, squares, inverse_t, upper1, upper2, upper3,
+                 raw_first, raw_near, raw_far):
     me, core, deep, plane = place()
     loads = [
         pltpu.make_async_copy(pivots_hbm, pivots_ref, loaded.at[0]),
@@ -402,127 +405,98 @@
     for copy in copies1 + copies2 + copies3:
         copy.wait_send()
 
-
-def gather(pivots, embed, amp):
-    return pl.pallas_call(
-        gather_kernel,
-        out_shape=(jax.ShapeDtypeStruct((4096, 256), BF16), jax.ShapeDtypeStruct((512, 128), F32)),
+    prepare(chosen_ref[...], matrix, pivots_t)
+    sums = factorise(features_ref, amp_ref, matrix, pivots_t, kern, cross, done, squares, inverse_t,
+                     (None, upper1, upper2, upper3), raw_first, raw_near, raw_far, factor_ref, residual_ref)
+
+    lane8 = lax.broadcasted_iota(jnp.int32, (8, 128), 1)
+    total = jnp.sum(amp_ref[...] * amp_ref[...])
+    value = jnp.zeros((8, 128), F32)
+    for p in range(4):
+        total = total - jnp.sum(sums[p])
+        value = jnp.where(lane8 == p, total, value)
+
+    mine1[core] = value
+    copy = pltpu.make_async_remote_copy(
+        src_ref=mine1.at[core], dst_ref=mine1.at[core], send_sem=total_sems.at[0], recv_sem=total_sems.at[1],
+        device_id=(other,), device_id_type=MESH)
+    copy.start()
+    copy.wait_recv()
+    value = mine1[0] + mine1[1]
+    copies4 = [copy]
+
+    def exchange(value, source, land, at, size, peers, first):
+        source[...] = value
+        land[at] = value
+        copies = []
+        for d in range(1, size):
+            copy = pltpu.make_async_remote_copy(
+                src_ref=source, dst_ref=land.at[at], send_sem=total_sems.at[first + d],
+                recv_sem=total_sems.at[first + size + at], device_id=(peers[d - 1],), device_id_type=MESH)
+            copy.start()
+            copies.append(copy)
+        for d in range(1, size):
+            origin = lax.rem(at + d, size)
+            pltpu.make_async_remote_copy(
+                src_ref=source, dst_ref=land.at[origin], send_sem=total_sems.at[first + d],
+                recv_sem=total_sems.at[first + size + origin], device_id=(peers[d - 1],),
+                device_id_type=MESH).wait_recv()
+        return copies, jnp.sum(land[...], axis=0)
+
+    copies5, value = exchange(value, mine2, land2, deep, 8, peers1, 2)
+    copies6, value = exchange(value, mine3, land3, plane, 16, peers2, 18)
+    means_ref[...] = value[0:1, 0:4] * (1.0 / points)
+    for copy in copies4 + copies5 + copies6:
+        copy.wait_send()
+
+
+def write_kernel(factor_ref, residual_ref, means_ref, factor_hbm, residual_hbm, means_hbm, sems):
+    copies = [
+        pltpu.make_async_copy(residual_ref, residual_hbm, sems.at[8]),
+        pltpu.make_async_copy(means_ref, means_hbm, sems.at[9]),
+    ]
+    for part in range(8):
+        rows = pl.ds(512 * part, 512)
+        copies.append(pltpu.make_async_copy(factor_ref.at[rows], factor_hbm.at[rows], sems.at[part]))
+    for copy in copies:
+        copy.start()
+    for copy in copies:
+        copy.wait()
+
+
+def local(embed, amplitude, pivots):
+    points = 4096 * lax.axis_size("rows")
+    factor, residual, means = pl.pallas_call(
+        functools.partial(whole_kernel, points),
+        out_shape=(jax.ShapeDtypeStruct((4096, 512), F32), jax.ShapeDtypeStruct((32, 128), F32),
+                   jax.ShapeDtypeStruct((1, 4), F32)),
         in_specs=[pl.BlockSpec(memory_space=pltpu.HBM)] * 3,
-        out_specs=(pl.BlockSpec(memory_space=pltpu.VMEM), pl.BlockSpec(memory_space=pltpu.VMEM)),
+        out_specs=[pl.BlockSpec(memory_space=pltpu.VMEM)] * 3,
         scratch_shapes=[
             pltpu.VMEM((4, 128), jnp.int32), pltpu.VMEM((64, 4096), F32), pltpu.VMEM((32, 128), F32),
             pltpu.SemaphoreType.DMA((3,)),
+            pltpu.VMEM((4096, 256), BF16), pltpu.VMEM((512, 128), F32),
             pltpu.VMEM((4, 128), F32), pltpu.VMEM((8, 4, 128), F32), pltpu.VMEM((4, 32, 8, 128), F32),
             pltpu.SemaphoreType.DMA((7,)), pltpu.SemaphoreType.DMA((8,)),
             pltpu.SemaphoreType.DMA((15,)), pltpu.SemaphoreType.DMA((16,)),
             pltpu.SemaphoreType.DMA((16,)), pltpu.SemaphoreType.DMA((16,)),
-        ],
-        compiler_params=pltpu.CompilerParams(collective_id=0, has_side_effects=True, vmem_limit_bytes=32 << 20),
-        name="gather_pivots",
-    )(pivots, embed, amp)
-
-
-def product_kernel(features_ref, chosen_ref, amp_ref, factor_ref, residual_ref, sums_ref,
-                   matrix, pivots_t, kern, cross, done, wide_amp, squares, inverse_t, upper1, upper2, upper3,
-                   raw_first, raw_near, raw_far, staged, sems):
-    prepare(chosen_ref[...], matrix, pivots_t)
-    copies = []
-
-    def sent(p, j):
-        if j % 4 == 3:
-            rows = pl.ds(CHUNK * (j - 3), 4 * CHUNK)
-            copy = pltpu.make_async_copy(
-                staged.at[p, rows], factor_ref.at[rows, pl.ds(128 * p, 128)], sems.at[4 * p + j // 4])
-            copy.start()
-            copies.append(copy)
-
-    sums = factorise(features_ref, amp_ref, matrix, pivots_t, kern, cross, done, wide_amp, squares, inverse_t,
-                     (None, upper1, upper2, upper3), raw_first, raw_near, raw_far, staged, residual_ref, sent)
-    for p in range(4):
-        sums_ref[8 * p:8 * p + 8, :] = sums[p]
-    for copy in copies:
-        copy.wait()
-
-
-def product(features, chosen, amp):
-    return pl.pallas_call(
-        product_kernel,
+            pltpu.VMEM((2, 8, 128), F32), pltpu.VMEM((8, 128), F32),
+            pltpu.VMEM((8, 8, 128), F32), pltpu.VMEM((8, 128), F32), pltpu.VMEM((16, 8, 128), F32),
+            pltpu.SemaphoreType.DMA((50,)),
+        ] + SCRATCH,
+        compiler_params=pltpu.CompilerParams(collective_id=0, has_side_effects=True, vmem_limit_bytes=45000000),
+        name="pivoted_cholesky",
+    )(pivots, embed.T, amplitude.reshape(32, 128))
+    factor, residual, means = pl.pallas_call(
+        write_kernel,
         out_shape=(jax.ShapeDtypeStruct((4096, 512), F32), jax.ShapeDtypeStruct((32, 128), F32),
-                   jax.ShapeDtypeStruct((32, 128), F32)),
+                   jax.ShapeDtypeStruct((1, 4), F32)),
         in_specs=[pl.BlockSpec(memory_space=pltpu.VMEM)] * 3,
-        out_specs=(pl.BlockSpec(memory_space=pltpu.HBM), pl.BlockSpec(memory_space=pltpu.VMEM),
-                   pl.BlockSpec(memory_space=pltpu.VMEM)),
-        scratch_shapes=SCRATCH + [pltpu.VMEM((4, 4096, 128), F32), pltpu.SemaphoreType.DMA((16,))],
-        compiler_params=pltpu.CompilerParams(vmem_limit_bytes=50 << 20),
-        name="cholesky_product",
-    )(features, chosen, amp)
-
-
-def sums_kernel(points, sums_ref, amp_ref, means_ref, own, land1, middle, land2, send1, recv1, send2, recv2):
-    me, core, deep, plane = place()
-    line = deep * 2 + core
-    barrier = pltpu.get_barrier_semaphore()
-    peers1 = [plane * 16 + lax.rem(line + d, 16) for d in range(1, 16)]
-    peers2 = [lax.rem(plane + d, 16) * 16 + line for d in range(1, 16)]
-    for peer in peers1 + peers2:
-        pl.semaphore_signal(barrier, inc=1, device_id=(peer,), device_id_type=MESH)
-
-    lane = lax.broadcasted_iota(jnp.int32, (8, 128), 1)
-    total = jnp.sum(amp_ref[...] * amp_ref[...])
-    value = jnp.zeros((8, 128), F32)
-    for p in range(4):
-        total = total - jnp.sum(sums_ref[8 * p:8 * p + 8, :])
-        value = jnp.where(lane == p, total, value)
-    own[...] = value
-    land1[line] = value
-    pl.semaphore_wait(barrier, 30)
-
-    def exchange(source, land, at, peers, send, recv):
-        copies = []
-        for d in range(1, 16):
-            copy = pltpu.make_async_remote_copy(
-                src_ref=source, dst_ref=land.at[at], send_sem=send.at[d - 1], recv_sem=recv.at[at],
-                device_id=(peers[d - 1],), device_id_type=MESH)
-            copy.start()
-            copies.append(copy)
-        for d in range(1, 16):
-            origin = lax.rem(at + d, 16)
-            pltpu.make_async_remote_copy(
-                src_ref=source, dst_ref=land.at[origin], send_sem=send.at[d - 1], recv_sem=recv.at[origin],
-                device_id=(peers[d - 1],), device_id_type=MESH).wait_recv()
-        return copies, jnp.sum(land[...], axis=0)
-
-    copies1, value = exchange(own, land1, line, peers1, send1, recv1)
-    middle[...] = value
-    land2[plane] = value
-    copies2, value = exchange(middle, land2, plane, peers2, send2, recv2)
-    means_ref[...] = value[0:1, 0:4] * (1.0 / points)
-    for copy in copies1 + copies2:
-        copy.wait_send()
-
-
-def mean_sums(sums, amp, points):
-    return pl.pallas_call(
-        functools.partial(sums_kernel, points),
-        out_shape=jax.ShapeDtypeStruct((1, 4), F32),
-        in_specs=[pl.BlockSpec(memory_space=pltpu.VMEM)] * 2,
-        out_specs=pl.BlockSpec(memory_space=pltpu.VMEM),
-        scratch_shapes=[
-            pltpu.VMEM((8, 128), F32), pltpu.VMEM((16, 8, 128), F32), pltpu.VMEM((8, 128), F32),
-            pltpu.VMEM((16, 8, 128), F32),
-            pltpu.SemaphoreType.DMA((15,)), pltpu.SemaphoreType.DMA((16,)),
-            pltpu.SemaphoreType.DMA((15,)), pltpu.SemaphoreType.DMA((16,)),
-        ],
-        compiler_params=pltpu.CompilerParams(collective_id=1, has_side_effects=True),
-        name="sum_residuals",
-    )(sums, amp)
-
-
-def local(embed, amplitude, pivots):
-    amp = amplitude.reshape(32, 128)
-    features, chosen = gather(pivots, embed.T, amp)
-    factor, residual, sums = product(features, chosen, amp)
-    means = mean_sums(sums, amp, 4096 * lax.axis_size("rows"))
+        out_specs=[pl.BlockSpec(memory_space=pltpu.HBM)] * 3,
+        scratch_shapes=[pltpu.SemaphoreType.DMA((10,))],
+        compiler_params=pltpu.CompilerParams(vmem_limit_bytes=1 << 20),
+        name="write_out",
+    )(factor, residual, means)
     return factor, residual.reshape(4096), means.reshape(4)
 
 

time: 62.1 us -> 55.4 us (0.89)
  Pallas kernels: 55.9 us -> 51.5 us
  local copies, waits for them, and re-layouts: 5.03 us -> 2.62 us
    pallas_call x3 -> x2, Pallas kernels: 55.9 us -> 51.5 us  [the longest x1 48.1 us: local(): pl.pallas_call(functools.partial(whole_kernel, points), out_shape=(jax.Sh...]
    unnamed x11 -> x6, local copies, waits for them, and re-layouts: 5.03 us -> 2.62 us
where the time goes in v3:
time: 55.4 us; the launch traced here: 54.9 us
  Pallas kernels  51.5 us (93%)
  local copies, waits for them, and re-layouts  2.62 us (5%)
  between operations  0.81 us (1%)
    pallas_call x1, Pallas kernels, local(): pl.pallas_call(functools.partial(whole_kernel, points), out_shape=(jax.Sh...  48.1 us
    pallas_call x1, Pallas kernels, local(): pl.pallas_call(write_kernel, out_shape=(jax.ShapeDtypeStruct((4096, 512),...  3.4 us
    unnamed x6, local copies, waits for them, and re-layouts  2.62 us

profile of v3, /device:TPU:1, one launch (start us, length us, event | category | flops | bytes accessed | tf_op | source)
XLA Modules:
  0.0 54.9 jit_solution(7863466864007607935)
XLA Ops:
  0.6 0.0 copy-start
  0.6 1.2 %copy-done = f32[4096,64]{0,1:T(8,128)S(1)} copy-done((f32[4096,64]{0,1:T(8,128)S(1)}, f32[4096,64]{0,1:T(8,128)}, u32[]{:S(2)}) %copy-start) | copy-done | bytes 1048600
  1.9 0.0 copy-start.1
  1.9 0.7 %copy-done.1 = f32[4096]{0:T(1024)S(1)} copy-done((f32[4096]{0:T(1024)S(1)}, f32[4096]{0:T(1024)}, u32[]{:S(2)}) %copy-start.1) | copy-done | bytes 16408
  2.6 0.0 copy-start.2
  2.6 0.7 %copy-done.2 = s32[4,128]{1,0:T(4,128)S(1)} copy-done((s32[4,128]{1,0:T(4,128)S(1)}, s32[4,128]{1,0:T(4,128)}, u32[]{:S(2)}) %copy-start.2) | copy-done | bytes 2072
  3.3 48.1 %pivoted_cholesky.1 = (f32[4096,512]{1,0:T(8,128)S(1)}, f32[32,128]{1,0:T(8,128)S(1)}, f32[1,4]{1,0:T(1,128)S(1)}) custom-call(s32[4,128]{1,0:T(4,128)S(1)} %copy-done.2, f32[64,4096]{1,0:T(8,128)S(1)} %bitcast.4, f32[32,128]{1,0:T(8,128)S(1)} %bitcast.5), custom_call_target="tpu_custom_call" | custom-call | tf_op jit(solution)/shard_map/pivoted_cholesky/pallas_call | solution.py:469
  51.4 3.4 %write_out.1 = (f32[4096,512]{1,0:T(8,128)}, f32[32,128]{1,0:T(8,128)}, f32[1,4]{1,0:T(1,128)}) custom-call(f32[4096,512]{1,0:T(8,128)S(1)} %get-tuple-element.9.factor_ref, f32[32,128]{1,0:T(8,128)S(1)} %get-tuple-element.10.residual_ref, f32[1,4]{1,0:T(1,128)S(1)} %get-tuple-element.11.means_ref), custom_call_target="tpu_custom_call" | custom-call | tf_op jit(solution)/shard_map/write_out/pallas_call | solution.py:490
Async XLA Ops:
  0.6 1.2 %copy-start = (f32[4096,64]{0,1:T(8,128)S(1)}, f32[4096,64]{0,1:T(8,128)}, u32[]{:S(2)}) copy-start(f32[4096,64]{0,1:T(8,128)} %param.3) | copy-start | bytes 3145732
  1.9 0.7 %copy-start.1 = (f32[4096]{0:T(1024)S(1)}, f32[4096]{0:T(1024)}, u32[]{:S(2)}) copy-start(f32[4096]{0:T(1024)} %param.4) | copy-start | bytes 49156
  2.6 0.7 %copy-start.2 = (s32[4,128]{1,0:T(4,128)S(1)}, s32[4,128]{1,0:T(4,128)}, u32[]{:S(2)}) copy-start(s32[4,128]{1,0:T(4,128)} %pivots_hbm.1) | copy-start | bytes 6148

commit v4 on v3

--- a/solution.py
+++ b/solution.py
@@ -110,25 +110,44 @@
     return value[:, 0:128] + value[:, 128:256]
 
 
-def prepare(chosen, matrix, pivots_t):
-    lane = lax.broadcasted_iota(jnp.int32, (512, 128), 1)
-    squared = jnp.sum(chosen * chosen, axis=1, keepdims=True) * (LOG2E / 64)
-    scaled = chosen * (2 * LOG2E / 64)
-    left = jnp.where(lane < 64, chosen, jnp.where(lane == 64, squared, jnp.where(lane == 65, 1.0, 0.0)))
-    right = jnp.where(lane < 64, scaled, jnp.where(lane == 64, -1.0, jnp.where(lane == 65, -squared, 0.0)))
-    power = lax.dot_general(left, right, (((1,), (1,)), ((), ())), precision=HI, preferred_element_type=F32)
-    matrix[...] = jnp.exp2(jnp.minimum(power, 0.0))
-    high, low = [v.astype(F32) for v in split_two(scaled)]
-    extra = [jnp.full((512, 1), -1.0, F32)] * 3 + [-v.astype(F32) for v in split_three(squared)]
-    extra += [jnp.full((512, 1), 1.0, F32)] * 3
-    one = jnp.where(lane < 64, high, pltpu.roll(high, 64, 1))
-    two = jnp.where(lane < 64, low, 0.0)
-    for index, value in enumerate(extra):
-        two = jnp.where(lane == 64 + index, value, two)
-    pivots_t[0:128, 0:512] = one.T.astype(BF16)
-    pivots_t[128:256, 0:512] = two.T.astype(BF16)
+def prepare(chosen_ref, matrix, pivots_t):
+    lane = lax.broadcasted_iota(jnp.int32, (128, 128), 1)
+    lefts, rights = [], []
+
+    def beside(first, second):
+        return jnp.where(lane < 64, first, pltpu.roll(second, 64, 1))
+
+    def with_tail(first, values):
+        out = jnp.where(lane < 64, first, 0.0)
+        for index, value in enumerate(values):
+            out = jnp.where(lane == 64 + index, value, out)
+        return out
+
+    def block(p, q, size):
+        right = jnp.concatenate(rights[q:q + size], axis=0)
+        power = lax.dot_general(lefts[p], right, (((1,), (1,)), ((), ())), preferred_element_type=F32)
+        matrix[128 * p:128 * p + 128, 128 * q:128 * (q + size)] = jnp.exp2(jnp.minimum(power, 0.0))
+
+    for p in range(4):
+        at = slice(128 * p, 128 * p + 128)
+        chosen = chosen_ref[at, :]
+        squared = jnp.sum(chosen * chosen, axis=1, keepdims=True) * (LOG2E / 64)
+        squares = [part.astype(F32) for part in split_three(squared)]
+        high, middle, low = [part.astype(F32) for part in split_three(chosen)]
+        left = [beside(high, middle), with_tail(high, squares + [1.0] * 3), beside(middle, high), with_tail(low, [])]
+        lefts.append(jnp.concatenate([part.astype(BF16) for part in left], axis=1))
+        high, middle, low = [part.astype(F32) for part in split_three(chosen * (2 * LOG2E / 64))]
+        one = beside(high, high)
+        two = with_tail(middle, [-1.0] * 3 + [-part for part in squares] + [1.0] * 3)
+        right = [one, two, beside(middle, low), with_tail(high, [])]
+        rights.append(jnp.concatenate([part.astype(BF16) for part in right], axis=1))
+        if p == 0:
+            block(0, 0, 1)
+        pivots_t[0:128, at] = one.T.astype(BF16)
+        pivots_t[128:256, at] = two.T.astype(BF16)
     row = lax.broadcasted_iota(jnp.int32, (256, 128), 0)
     pivots_t[:, 512:640] = jnp.where((row >= 198) & (row < 201), 1.0, 0.0).astype(BF16)
+    return [functools.partial(block, *which) for which in ((0, 1, 3), (1, 1, 3), (2, 2, 2), (3, 3, 1))]
 
 
 CHUNK = 256
@@ -138,7 +157,7 @@
 
 
 def factorise(features_ref, amp_ref, matrix, pivots_t, kern, cross, done, squares, inverse_t, upper,
-              raw_first, raw_near, raw_far, factor_ref, residual_ref):
+              raw_first, raw_near, raw_far, factor_ref, residual_ref, later):
     sums = [[] for _ in range(4)]
     pending = []
 
@@ -217,19 +236,28 @@
             step(len(pending))
             if j < 15:
                 schedule(16 * p + j + 1)
+            if j >= 8 and later:
+                pending.append(later.pop(0))
 
         schedule(16 * p)
         got = eliminate([matrix[lo + 8 * b:lo + 8 * b + 8, lo:lo + 128] for b in range(16)], work, step)
         inverse = jnp.where(lane <= sub, jnp.concatenate(got, axis=0), 0.0)
         inverse_t[p] = both_parts(inverse.T)
+        parts = {}
+
+        def extend(p, q, inverse, parts):
+            part = jnp.dot(inverse, matrix[128 * p:128 * p + 128, 128 * q:128 * q + 128],
+                           precision=HI, preferred_element_type=F32)
+            parts[q] = part
+            for r in range(p + 1, q + 1):
+                matrix[128 * r:128 * r + 128, 128 * q:128 * q + 128] -= lax.dot_general(
+                    parts[r], part, (((0,), (0,)), ((), ())), precision=HI, preferred_element_type=F32)
+            upper[q][256 * p:256 * p + 256, :] = both_parts(part)
+
         if p < 3:
-            right = jnp.dot(inverse, matrix[lo:lo + 128, lo + 128:], precision=HI, preferred_element_type=F32)
-            for q in range(p + 1, 4):
-                part = right[:, 128 * (q - p - 1):128 * (q - p)]
-                matrix[128 * q:128 * q + 128, 128 * q:] -= lax.dot_general(
-                    part, right[:, 128 * (q - p - 1):], (((0,), (0,)), ((), ())), precision=HI,
-                    preferred_element_type=F32)
-                upper[q][256 * p:256 * p + 256, :] = both_parts(part)
+            extend(p, p + 1, inverse, parts)
+        inverse_t[p] = both_parts(inverse.T)
+        later.extend(functools.partial(extend, p, q, inverse, parts) for q in range(p + 2, 4))
     for t in range(64, 82):
         schedule(t)
         step(len(pending))
@@ -243,6 +271,14 @@
     pltpu.VMEM((256, 256), BF16), pltpu.VMEM((512, 256), BF16), pltpu.VMEM((768, 256), BF16),
     pltpu.VMEM((2, CHUNK, 640), F32), pltpu.VMEM((2, CHUNK, 256), F32), pltpu.VMEM((2, CHUNK, 256), F32),
 ]
+
+
+def far_first():
+    found = [(min(y, 4 - y) + min(x, 4 - x) + min(z, 8 - z), y, x, z) for y in range(4) for x in range(4) for z in range(8)]
+    return [offset[1:] for offset in sorted(found, key=lambda offset: -offset[0])][:-1]
+
+
+FAR_FIRST = far_first()
 
 
 def place():
@@ -277,7 +313,7 @@
 def whole_kernel(points, pivots_hbm, embed_hbm, amp_hbm, factor_ref, residual_ref, means_ref,
                  pivots_ref, embed_ref, amp_ref, loaded, features_ref, chosen_ref,
                  own, column, whole, send1, recv1, send2, recv2, send3, recv3,
-                 mine1, mine2, land2, mine3, land3, total_sems,
+                 mine1, mine2, land2, total_sems,
                  matrix, pivots_t, kern, cross, done, squares, inverse_t, upper1, upper2, upper3,
                  raw_first, raw_near, raw_far):
     me, core, deep, plane = place()
@@ -405,9 +441,9 @@
     for copy in copies1 + copies2 + copies3:
         copy.wait_send()
 
-    prepare(chosen_ref[...], matrix, pivots_t)
+    later = prepare(chosen_ref, matrix, pivots_t)
     sums = factorise(features_ref, amp_ref, matrix, pivots_t, kern, cross, done, squares, inverse_t,
-                     (None, upper1, upper2, upper3), raw_first, raw_near, raw_far, factor_ref, residual_ref)
+                     (None, upper1, upper2, upper3), raw_first, raw_near, raw_far, factor_ref, residual_ref, later)
 
     lane8 = lax.broadcasted_iota(jnp.int32, (8, 128), 1)
     total = jnp.sum(amp_ref[...] * amp_ref[...])
@@ -422,32 +458,25 @@
         device_id=(other,), device_id_type=MESH)
     copy.start()
     copy.wait_recv()
-    value = mine1[0] + mine1[1]
-    copies4 = [copy]
-
-    def exchange(value, source, land, at, size, peers, first):
-        source[...] = value
-        land[at] = value
-        copies = []
-        for d in range(1, size):
-            copy = pltpu.make_async_remote_copy(
-                src_ref=source, dst_ref=land.at[at], send_sem=total_sems.at[first + d],
-                recv_sem=total_sems.at[first + size + at], device_id=(peers[d - 1],), device_id_type=MESH)
-            copy.start()
-            copies.append(copy)
-        for d in range(1, size):
-            origin = lax.rem(at + d, size)
-            pltpu.make_async_remote_copy(
-                src_ref=source, dst_ref=land.at[origin], send_sem=total_sems.at[first + d],
-                recv_sem=total_sems.at[first + size + origin], device_id=(peers[d - 1],),
-                device_id_type=MESH).wait_recv()
-        return copies, jnp.sum(land[...], axis=0)
-
-    copies5, value = exchange(value, mine2, land2, deep, 8, peers1, 2)
-    copies6, value = exchange(value, mine3, land3, plane, 16, peers2, 18)
-    means_ref[...] = value[0:1, 0:4] * (1.0 / points)
-    for copy in copies4 + copies5 + copies6:
-        copy.wait_send()
+    chips = plane * 8 + deep
+    mine2[...] = mine1[0, 0:1, :] + mine1[1, 0:1, :]
+    land2[chips] = mine2[...]
+    high, wide = plane // 4, lax.rem(plane, 4)
+    targets = []
+    for dy, dx, dz in FAR_FIRST:
+        there = lax.rem(high + dy, 4) * 4 + lax.rem(wide + dx, 4)
+        targets.append(device_of(there, lax.rem(deep + dz, 8), core))
+    for target in targets:
+        pltpu.make_async_remote_copy(
+            src_ref=mine2, dst_ref=land2.at[chips], send_sem=total_sems.at[2], recv_sem=total_sems.at[3],
+            device_id=(target,), device_id_type=MESH).start()
+    every = pltpu.make_async_remote_copy(
+        src_ref=land2.at[0:127], dst_ref=land2.at[0:127], send_sem=total_sems.at[2], recv_sem=total_sems.at[3],
+        device_id=(targets[0],), device_id_type=MESH)
+    every.wait_recv()
+    means_ref[...] = jnp.sum(land2[...], axis=0)[:, 0:4] * (1.0 / points)
+    copy.wait_send()
+    every.wait_send()
 
 
 def write_kernel(factor_ref, residual_ref, means_ref, factor_hbm, residual_hbm, means_hbm, sems):
@@ -480,9 +509,8 @@
             pltpu.SemaphoreType.DMA((7,)), pltpu.SemaphoreType.DMA((8,)),
             pltpu.SemaphoreType.DMA((15,)), pltpu.SemaphoreType.DMA((16,)),
             pltpu.SemaphoreType.DMA((16,)), pltpu.SemaphoreType.DMA((16,)),
-            pltpu.VMEM((2, 8, 128), F32), pltpu.VMEM((8, 128), F32),
-            pltpu.VMEM((8, 8, 128), F32), pltpu.VMEM((8, 128), F32), pltpu.VMEM((16, 8, 128), F32),
-            pltpu.SemaphoreType.DMA((50,)),
+            pltpu.VMEM((2, 8, 128), F32), pltpu.VMEM((1, 128), F32), pltpu.VMEM((128, 1, 128), F32),
+            pltpu.SemaphoreType.DMA((4,)),
         ] + SCRATCH,
         compiler_params=pltpu.CompilerParams(collective_id=0, has_side_effects=True, vmem_limit_bytes=45000000),
         name="pivoted_cholesky",

time: 55.4 us -> 52.9 us (0.955)
  Pallas kernels: 51.5 us -> 49.3 us
    pallas_call x1, Pallas kernels: 48.1 us -> 45.9 us  [local(): pl.pallas_call(functools.partial(whole_kernel, points), out_shape=(jax.Sh...]
where the time goes in v4:
time: 52.9 us; the launch traced here: 52.7 us
  Pallas kernels  49.3 us (93%)
  local copies, waits for them, and re-layouts  2.62 us (5%)
  between operations  0.81 us (2%)
    pallas_call x1, Pallas kernels, local(): pl.pallas_call(functools.partial(whole_kernel, points), out_shape=(jax.Sh...  45.9 us
    pallas_call x1, Pallas kernels, local(): pl.pallas_call(write_kernel, out_shape=(jax.ShapeDtypeStruct((4096, 512),...  3.4 us
    unnamed x6, local copies, waits for them, and re-layouts  2.62 us

profile of v4, /device:TPU:1, one launch (start us, length us, event | category | flops | bytes accessed | tf_op | source)
XLA Modules:
  0.0 52.7 jit_solution(5748023277049603363)
XLA Ops:
  0.6 0.0 copy-start
  0.6 1.2 %copy-done = f32[4096,64]{0,1:T(8,128)S(1)} copy-done((f32[4096,64]{0,1:T(8,128)S(1)}, f32[4096,64]{0,1:T(8,128)}, u32[]{:S(2)}) %copy-start) | copy-done | bytes 1048600
  1.9 0.0 copy-start.1
  1.9 0.7 %copy-done.1 = f32[4096]{0:T(1024)S(1)} copy-done((f32[4096]{0:T(1024)S(1)}, f32[4096]{0:T(1024)}, u32[]{:S(2)}) %copy-start.1) | copy-done | bytes 16408
  2.6 0.0 copy-start.2
  2.6 0.7 %copy-done.2 = s32[4,128]{1,0:T(4,128)S(1)} copy-done((s32[4,128]{1,0:T(4,128)S(1)}, s32[4,128]{1,0:T(4,128)}, u32[]{:S(2)}) %copy-start.2) | copy-done | bytes 2072
  3.3 45.9 %pivoted_cholesky.1 = (f32[4096,512]{1,0:T(8,128)S(1)}, f32[32,128]{1,0:T(8,128)S(1)}, f32[1,4]{1,0:T(1,128)S(1)}) custom-call(s32[4,128]{1,0:T(4,128)S(1)} %copy-done.2, f32[64,4096]{1,0:T(8,128)S(1)} %bitcast.4, f32[32,128]{1,0:T(8,128)S(1)} %bitcast.5), custom_call_target="tpu_custom_call" | custom-call | tf_op jit(solution)/shard_map/pivoted_cholesky/pallas_call | solution.py:498
  49.1 3.4 %write_out.1 = (f32[4096,512]{1,0:T(8,128)}, f32[32,128]{1,0:T(8,128)}, f32[1,4]{1,0:T(1,128)}) custom-call(f32[4096,512]{1,0:T(8,128)S(1)} %get-tuple-element.9.factor_ref, f32[32,128]{1,0:T(8,128)S(1)} %get-tuple-element.10.residual_ref, f32[1,4]{1,0:T(1,128)S(1)} %get-tuple-element.11.means_ref), custom_call_target="tpu_custom_call" | custom-call | tf_op jit(solution)/shard_map/write_out/pallas_call | solution.py:518
Async XLA Ops:
  0.6 1.2 %copy-start = (f32[4096,64]{0,1:T(8,128)S(1)}, f32[4096,64]{0,1:T(8,128)}, u32[]{:S(2)}) copy-start(f32[4096,64]{0,1:T(8,128)} %param.3) | copy-start | bytes 3145732
  1.9 0.7 %copy-start.1 = (f32[4096]{0:T(1024)S(1)}, f32[4096]{0:T(1024)}, u32[]{:S(2)}) copy-start(f32[4096]{0:T(1024)} %param.4) | copy-start | bytes 49156
  2.6 0.7 %copy-start.2 = (s32[4,128]{1,0:T(4,128)S(1)}, s32[4,128]{1,0:T(4,128)}, u32[]{:S(2)}) copy-start(s32[4,128]{1,0:T(4,128)} %pivots_hbm.1) | copy-start | bytes 6148

commit v5 on v4

--- a/solution.py
+++ b/solution.py
@@ -274,8 +274,11 @@
 
 
 def far_first():
-    found = [(min(y, 4 - y) + min(x, 4 - x) + min(z, 8 - z), y, x, z) for y in range(4) for x in range(4) for z in range(8)]
-    return [offset[1:] for offset in sorted(found, key=lambda offset: -offset[0])][:-1]
+    found = [
+        (min(y, 4 - y) + min(x, 4 - x) + min(z, 8 - z), y, x, z, c)
+        for y in range(4) for x in range(4) for z in range(8) for c in range(2)
+    ]
+    return [offset[1:] for offset in sorted(found, key=lambda offset: (-offset[0], -offset[4]))][:-1]
 
 
 FAR_FIRST = far_first()
@@ -313,7 +316,7 @@
 def whole_kernel(points, pivots_hbm, embed_hbm, amp_hbm, factor_ref, residual_ref, means_ref,
                  pivots_ref, embed_ref, amp_ref, loaded, features_ref, chosen_ref,
                  own, column, whole, send1, recv1, send2, recv2, send3, recv3,
-                 mine1, mine2, land2, total_sems,
+                 my_sums, all_sums, total_sems,
                  matrix, pivots_t, kern, cross, done, squares, inverse_t, upper1, upper2, upper3,
                  raw_first, raw_near, raw_far):
     me, core, deep, plane = place()
@@ -452,30 +455,22 @@
         total = total - jnp.sum(sums[p])
         value = jnp.where(lane8 == p, total, value)
 
-    mine1[core] = value
-    copy = pltpu.make_async_remote_copy(
-        src_ref=mine1.at[core], dst_ref=mine1.at[core], send_sem=total_sems.at[0], recv_sem=total_sems.at[1],
-        device_id=(other,), device_id_type=MESH)
-    copy.start()
-    copy.wait_recv()
-    chips = plane * 8 + deep
-    mine2[...] = mine1[0, 0:1, :] + mine1[1, 0:1, :]
-    land2[chips] = mine2[...]
+    my_sums[...] = value[0:1, :]
+    all_sums[me] = my_sums[...]
     high, wide = plane // 4, lax.rem(plane, 4)
     targets = []
-    for dy, dx, dz in FAR_FIRST:
+    for dy, dx, dz, dc in FAR_FIRST:
         there = lax.rem(high + dy, 4) * 4 + lax.rem(wide + dx, 4)
-        targets.append(device_of(there, lax.rem(deep + dz, 8), core))
+        targets.append(device_of(there, lax.rem(deep + dz, 8), lax.rem(core + dc, 2)))
     for target in targets:
         pltpu.make_async_remote_copy(
-            src_ref=mine2, dst_ref=land2.at[chips], send_sem=total_sems.at[2], recv_sem=total_sems.at[3],
+            src_ref=my_sums, dst_ref=all_sums.at[me], send_sem=total_sems.at[0], recv_sem=total_sems.at[1],
             device_id=(target,), device_id_type=MESH).start()
     every = pltpu.make_async_remote_copy(
-        src_ref=land2.at[0:127], dst_ref=land2.at[0:127], send_sem=total_sems.at[2], recv_sem=total_sems.at[3],
+        src_ref=all_sums.at[0:255], dst_ref=all_sums.at[0:255], send_sem=total_sems.at[0], recv_sem=total_sems.at[1],
         device_id=(targets[0],), device_id_type=MESH)
     every.wait_recv()
-    means_ref[...] = jnp.sum(land2[...], axis=0)[:, 0:4] * (1.0 / points)
-    copy.wait_send()
+    means_ref[...] = jnp.sum(all_sums[...], axis=0)[:, 0:4] * (1.0 / points)
     every.wait_send()
 
 
@@ -495,6 +490,10 @@
 
 def local(embed, amplitude, pivots):
     points = 4096 * lax.axis_size("rows")
+    operands = [
+        pltpu.with_memory_space_constraint(value, pltpu.HBM)
+        for value in (pivots, embed.T, amplitude.reshape(32, 128))
+    ]
     factor, residual, means = pl.pallas_call(
         functools.partial(whole_kernel, points),
         out_shape=(jax.ShapeDtypeStruct((4096, 512), F32), jax.ShapeDtypeStruct((32, 128), F32),
@@ -509,12 +508,11 @@
             pltpu.SemaphoreType.DMA((7,)), pltpu.SemaphoreType.DMA((8,)),
             pltpu.SemaphoreType.DMA((15,)), pltpu.SemaphoreType.DMA((16,)),
             pltpu.SemaphoreType.DMA((16,)), pltpu.SemaphoreType.DMA((16,)),
-            pltpu.VMEM((2, 8, 128), F32), pltpu.VMEM((1, 128), F32), pltpu.VMEM((128, 1, 128), F32),
-            pltpu.SemaphoreType.DMA((4,)),
+            pltpu.VMEM((1, 128), F32), pltpu.VMEM((256, 1, 128), F32), pltpu.SemaphoreType.DMA((2,)),
         ] + SCRATCH,
         compiler_params=pltpu.CompilerParams(collective_id=0, has_side_effects=True, vmem_limit_bytes=45000000),
         name="pivoted_cholesky",
-    )(pivots, embed.T, amplitude.reshape(32, 128))
+    )(*operands)
     factor, residual, means = pl.pallas_call(
         write_kernel,
         out_shape=(jax.ShapeDtypeStruct((4096, 512), F32), jax.ShapeDtypeStruct((32, 128), F32),

time: 52.9 us -> 51.6 us (0.975)
  local copies, waits for them, and re-layouts: 2.62 us -> 0 us
  Pallas kernels: 49.3 us -> 50.7 us
    unnamed x6 -> x0, local copies, waits for them, and re-layouts: 2.62 us -> none
    pallas_call x1, Pallas kernels: 45.9 us -> 47.3 us  [local(): pl.pallas_call(functools.partial(whole_kernel, points), out_shape=(jax.Sh...]
where the time goes in v5:
time: 51.6 us; the launch traced here: 51.5 us
  Pallas kernels  50.7 us (98%)
  between operations  0.8 us (2%)
    pallas_call x1, Pallas kernels, local(): pl.pallas_call(functools.partial(whole_kernel, points), out_shape=(jax.Sh...  47.3 us
    pallas_call x1, Pallas kernels, local(): pl.pallas_call(write_kernel, out_shape=(jax.ShapeDtypeStruct((4096, 512),...  3.4 us

profile of v5, /device:TPU:1, one launch (start us, length us, event | category | flops | bytes accessed | tf_op | source)
XLA Modules:
  0.0 51.5 jit_solution(2572491197821162682)
XLA Ops:
  0.6 47.3 %pivoted_cholesky.1 = (f32[4096,512]{1,0:T(8,128)S(1)}, f32[32,128]{1,0:T(8,128)S(1)}, f32[1,4]{1,0:T(1,128)S(1)}) custom-call(s32[4,128]{1,0:T(4,128)} %pivots_hbm.1, f32[64,4096]{1,0:T(8,128)} %bitcast.4, f32[32,128]{1,0:T(8,128)} %bitcast.5), custom_call_target="tpu_custom_call" | custom-call | tf_op jit(solution)/shard_map/pivoted_cholesky/pallas_call | solution.py:497
  47.9 3.4 %write_out.1 = (f32[4096,512]{1,0:T(8,128)}, f32[32,128]{1,0:T(8,128)}, f32[1,4]{1,0:T(1,128)}) custom-call(f32[4096,512]{1,0:T(8,128)S(1)} %get-tuple-element.9.factor_ref, f32[32,128]{1,0:T(8,128)S(1)} %get-tuple-element.10.residual_ref, f32[1,4]{1,0:T(1,128)S(1)} %get-tuple-element.11.means_ref), custom_call_target="tpu_custom_call" | custom-call | tf_op jit(solution)/shard_map/write_out/pallas_call | solution.py:516

commit v6 on v5

--- a/solution.py
+++ b/solution.py
@@ -110,7 +110,7 @@
     return value[:, 0:128] + value[:, 128:256]
 
 
-def prepare(chosen_ref, matrix, pivots_t):
+def prepare(pick, matrix, pivots_t):
     lane = lax.broadcasted_iota(jnp.int32, (128, 128), 1)
     lefts, rights = [], []
 
@@ -130,7 +130,7 @@
 
     for p in range(4):
         at = slice(128 * p, 128 * p + 128)
-        chosen = chosen_ref[at, :]
+        chosen = pick(p)
         squared = jnp.sum(chosen * chosen, axis=1, keepdims=True) * (LOG2E / 64)
         squares = [part.astype(F32) for part in split_three(squared)]
         high, middle, low = [part.astype(F32) for part in split_three(chosen)]
@@ -157,7 +157,7 @@
 
 
 def factorise(features_ref, amp_ref, matrix, pivots_t, kern, cross, done, squares, inverse_t, upper,
-              raw_first, raw_near, raw_far, factor_ref, residual_ref, later):
+              raw_first, raw_near, raw_far, factor_ref, later):
     sums = [[] for _ in range(4)]
     pending = []
 
@@ -190,8 +190,6 @@
         if p < 3:
             squares[at, :] = square if p == 0 else squares[at, :] + square
             done[at, 256 * p:256 * p + 256] = jnp.concatenate(split_two(got), axis=1)
-        else:
-            squares[at, :] = squares[at, :] + square
 
     def start_far(p, j):
         raw_far[j % 2] = jnp.dot(
@@ -200,14 +198,6 @@
     def end_far(p, j, at, part):
         rest = kern[at, 128 * p:128 * p + 128] - halves(raw_far[j % 2, part, :])
         cross[at, :] = jnp.concatenate(split_two(rest), axis=1)
-
-    def residual_of(j):
-        both = jnp.concatenate(split_two(squares[CHUNK * j:CHUNK * j + CHUNK, :]), axis=1)
-        spent = lax.dot_general(jnp.ones((8, 256), BF16), both, (((1,), (1,)), ((), ())), preferred_element_type=F32)
-        for b in range(CHUNK // 128):
-            row = j * (CHUNK // 128) + b
-            own = amp_ref[row:row + 1, :]
-            residual_ref[row:row + 1, :] = own * own - spent[0:1, 128 * b:128 * b + 128]
 
     def schedule(t):
         if 0 <= t < 16:
@@ -224,8 +214,6 @@
             pending.extend(functools.partial(end_near, p, j, *piece) for piece in pieces(j))
             if p < 3:
                 pending.append(functools.partial(start_far, p, j))
-        if 66 <= t < 82:
-            pending.append(functools.partial(residual_of, t - 66))
 
     lane = lax.broadcasted_iota(jnp.int32, (128, 128), 1)
     sub = lax.broadcasted_iota(jnp.int32, (128, 128), 0)
@@ -258,10 +246,22 @@
             extend(p, p + 1, inverse, parts)
         inverse_t[p] = both_parts(inverse.T)
         later.extend(functools.partial(extend, p, q, inverse, parts) for q in range(p + 2, 4))
-    for t in range(64, 82):
+    for t in range(64, 81):
         schedule(t)
         step(len(pending))
     return [tree(parts) for parts in sums]
+
+
+def residuals(amp_ref, squares, factor_ref, residual_ref):
+    for j in range(CHUNKS):
+        at = slice(CHUNK * j, CHUNK * j + CHUNK)
+        last = factor_ref[at, 384:512]
+        both = jnp.concatenate(split_two(squares[at, :] + last * last), axis=1)
+        spent = lax.dot_general(jnp.ones((8, 256), BF16), both, (((1,), (1,)), ((), ())), preferred_element_type=F32)
+        for b in range(CHUNK // 128):
+            row = j * (CHUNK // 128) + b
+            own = amp_ref[row:row + 1, :]
+            residual_ref[row:row + 1, :] = own * own - spent[0:1, 128 * b:128 * b + 128]
 
 
 SCRATCH = [
@@ -314,7 +314,7 @@
 
 
 def whole_kernel(points, pivots_hbm, embed_hbm, amp_hbm, factor_ref, residual_ref, means_ref,
-                 pivots_ref, embed_ref, amp_ref, loaded, features_ref, chosen_ref,
+                 pivots_ref, embed_ref, amp_ref, loaded, features_ref,
                  own, column, whole, send1, recv1, send2, recv2, send3, recv3,
                  my_sums, all_sums, total_sems,
                  matrix, pivots_t, kern, cross, done, squares, inverse_t, upper1, upper2, upper3,
@@ -430,7 +430,7 @@
             src_ref=whole.at[:, at], dst_ref=whole.at[:, at], send_sem=send3.at[0], recv_sem=recv3.at[source],
             device_id=(other,), device_id_type=MESH).wait_recv()
 
-    for p in range(4):
+    def pick(p):
         spot, slot = wanted[p]
         rows = whole[p].reshape(256, 128)
         parts = jnp.concatenate(split_three(rows), axis=1)
@@ -439,21 +439,19 @@
         got = jnp.dot(take, parts, preferred_element_type=F32)
         got = got[:, 0:128] + (got[:, 128:256] + got[:, 256:384])
         got = jnp.where(slot > 0.5, pltpu.roll(got, 64, 1), got)
-        chosen_ref[128 * p:128 * p + 128, :] = jnp.where(lanes2 < 64, got, 0.0)
-
-    for copy in copies1 + copies2 + copies3:
-        copy.wait_send()
-
-    later = prepare(chosen_ref, matrix, pivots_t)
+        return jnp.where(lanes2 < 64, got, 0.0)
+
+    later = prepare(pick, matrix, pivots_t)
     sums = factorise(features_ref, amp_ref, matrix, pivots_t, kern, cross, done, squares, inverse_t,
-                     (None, upper1, upper2, upper3), raw_first, raw_near, raw_far, factor_ref, residual_ref, later)
+                     (None, upper1, upper2, upper3), raw_first, raw_near, raw_far, factor_ref, later)
 
     lane8 = lax.broadcasted_iota(jnp.int32, (8, 128), 1)
-    total = jnp.sum(amp_ref[...] * amp_ref[...])
+    own_squares = amp_ref[...] * amp_ref[...]
+    total = tree([own_squares[8 * b:8 * b + 8, :] for b in range(4)])
     value = jnp.zeros((8, 128), F32)
     for p in range(4):
-        total = total - jnp.sum(sums[p])
-        value = jnp.where(lane8 == p, total, value)
+        total = total - sums[p]
+        value = jnp.where(lane8 == p, jnp.sum(jnp.sum(total, axis=0, keepdims=True), axis=1, keepdims=True), value)
 
     my_sums[...] = value[0:1, :]
     all_sums[me] = my_sums[...]
@@ -469,9 +467,12 @@
     every = pltpu.make_async_remote_copy(
         src_ref=all_sums.at[0:255], dst_ref=all_sums.at[0:255], send_sem=total_sems.at[0], recv_sem=total_sems.at[1],
         device_id=(targets[0],), device_id_type=MESH)
+    residuals(amp_ref, squares, factor_ref, residual_ref)
     every.wait_recv()
     means_ref[...] = jnp.sum(all_sums[...], axis=0)[:, 0:4] * (1.0 / points)
     every.wait_send()
+    for copy in copies1 + copies2 + copies3:
+        copy.wait_send()
 
 
 def write_kernel(factor_ref, residual_ref, means_ref, factor_hbm, residual_hbm, means_hbm, sems):
@@ -503,7 +504,7 @@
         scratch_shapes=[
             pltpu.VMEM((4, 128), jnp.int32), pltpu.VMEM((64, 4096), F32), pltpu.VMEM((32, 128), F32),
             pltpu.SemaphoreType.DMA((3,)),
-            pltpu.VMEM((4096, 256), BF16), pltpu.VMEM((512, 128), F32),
+            pltpu.VMEM((4096, 256), BF16),
             pltpu.VMEM((4, 128), F32), pltpu.VMEM((8, 4, 128), F32), pltpu.VMEM((4, 32, 8, 128), F32),
             pltpu.SemaphoreType.DMA((7,)), pltpu.SemaphoreType.DMA((8,)),
             pltpu.SemaphoreType.DMA((15,)), pltpu.SemaphoreType.DMA((16,)),

time: 51.6 us -> 50.5 us (0.979)
  Pallas kernels: 50.7 us -> 49.6 us
    pallas_call x1, Pallas kernels: 47.3 us -> 46.2 us  [local(): pl.pallas_call(functools.partial(whole_kernel, points), out_shape=(jax.Sh...]
where the time goes in v6:
time: 50.5 us; the launch traced here: 50.4 us
  Pallas kernels  49.6 us (98%)
  between operations  0.8 us (2%)
    pallas_call x1, Pallas kernels, local(): pl.pallas_call(functools.partial(whole_kernel, points), out_shape=(jax.Sh...  46.2 us
    pallas_call x1, Pallas kernels, local(): pl.pallas_call(write_kernel, out_shape=(jax.ShapeDtypeStruct((4096, 512),...  3.4 us

profile of v6, /device:TPU:1, one launch (start us, length us, event | category | flops | bytes accessed | tf_op | source)
XLA Modules:
  0.0 50.4 jit_solution(1398341182050117928)
XLA Ops:
  0.6 46.2 %pivoted_cholesky.1 = (f32[4096,512]{1,0:T(8,128)S(1)}, f32[32,128]{1,0:T(8,128)S(1)}, f32[1,4]{1,0:T(1,128)S(1)}) custom-call(s32[4,128]{1,0:T(4,128)} %pivots_hbm.1, f32[64,4096]{1,0:T(8,128)} %bitcast.4, f32[32,128]{1,0:T(8,128)} %bitcast.5), custom_call_target="tpu_custom_call" | custom-call | tf_op jit(solution)/shard_map/pivoted_cholesky/pallas_call | solution.py:498
  46.9 3.4 %write_out.1 = (f32[4096,512]{1,0:T(8,128)}, f32[32,128]{1,0:T(8,128)}, f32[1,4]{1,0:T(1,128)}) custom-call(f32[4096,512]{1,0:T(8,128)S(1)} %get-tuple-element.9.factor_ref, f32[32,128]{1,0:T(8,128)S(1)} %get-tuple-element.10.residual_ref, f32[1,4]{1,0:T(1,128)S(1)} %get-tuple-element.11.means_ref), custom_call_target="tpu_custom_call" | custom-call | tf_op jit(solution)/shard_map/write_out/pallas_call | solution.py:517

commit v7 on v6

--- a/solution.py
+++ b/solution.py
@@ -282,6 +282,7 @@
 
 
 FAR_FIRST = far_first()
+PLANES_FAR_FIRST = [(dy, dx) for dy, dx, dz, dc in FAR_FIRST if dz == 0 and dc == 0]
 
 
 def place():
@@ -329,7 +330,9 @@
         load.start()
     barrier = pltpu.get_barrier_semaphore()
     peers1 = [device_of(plane, lax.rem(deep + d, 8), core) for d in range(1, 8)]
-    peers2 = [device_of(lax.rem(plane + d, 16), deep, core) for d in range(1, 16)]
+    turn = lambda dy, dx: lax.rem(plane // 4 + dy, 4) * 4 + lax.rem(lax.rem(plane, 4) + dx, 4)
+    planes = [turn(dy, dx) for dy, dx in PLANES_FAR_FIRST]
+    peers2 = [device_of(there, deep, core) for there in planes]
     other = device_of(plane, deep, 1 - core)
     for peer in peers1 + peers2 + [other]:
         pl.semaphore_signal(barrier, inc=1, device_id=(peer,), device_id_type=MESH)
@@ -364,7 +367,7 @@
     pl.semaphore_wait(barrier, 23)
 
     copies1 = []
-    for d in range(1, 8):
+    for d in (4, 3, 5, 2, 6, 1, 7):
         copy = pltpu.make_async_remote_copy(
             src_ref=own, dst_ref=column.at[deep], send_sem=send1.at[d - 1], recv_sem=recv1.at[deep],
             device_id=(peers1[d - 1],), device_id_type=MESH)
@@ -417,8 +420,8 @@
         features_ref[start:start + 128, 0:128] = one
         features_ref[start:start + 128, 128:256] = two
 
-    for d in range(1, 16):
-        source = lax.rem(plane + d, 16)
+    for d in range(15, 0, -1):
+        source = planes[d - 1]
         at = core * 16 + source
         pltpu.make_async_remote_copy(
             src_ref=whole.at[:, at], dst_ref=whole.at[:, at], send_sem=send2.at[d - 1], recv_sem=recv2.at[source],

time: 50.5 us -> 50.1 us (level)
  no operation moved by 1% of the time
where the time goes in v7:
time: 50.1 us; the launch traced here: 50 us
  Pallas kernels  49.2 us (98%)
  between operations  0.8 us (2%)
    pallas_call x1, Pallas kernels, local(): pl.pallas_call(functools.partial(whole_kernel, points), out_shape=(jax.Sh...  45.8 us
    pallas_call x1, Pallas kernels, local(): pl.pallas_call(write_kernel, out_shape=(jax.ShapeDtypeStruct((4096, 512),...  3.4 us

profile of v7, /device:TPU:1, one launch (start us, length us, event | category | flops | bytes accessed | tf_op | source)
XLA Modules:
  0.0 50.0 jit_solution(5059632056332811155)
XLA Ops:
  0.6 45.8 %pivoted_cholesky.1 = (f32[4096,512]{1,0:T(8,128)S(1)}, f32[32,128]{1,0:T(8,128)S(1)}, f32[1,4]{1,0:T(1,128)S(1)}) custom-call(s32[4,128]{1,0:T(4,128)} %pivots_hbm.1, f32[64,4096]{1,0:T(8,128)} %bitcast.4, f32[32,128]{1,0:T(8,128)} %bitcast.5), custom_call_target="tpu_custom_call" | custom-call | tf_op jit(solution)/shard_map/pivoted_cholesky/pallas_call | solution.py:501
  46.5 3.4 %write_out.1 = (f32[4096,512]{1,0:T(8,128)}, f32[32,128]{1,0:T(8,128)}, f32[1,4]{1,0:T(1,128)}) custom-call(f32[4096,512]{1,0:T(8,128)S(1)} %get-tuple-element.9.factor_ref, f32[32,128]{1,0:T(8,128)S(1)} %get-tuple-element.10.residual_ref, f32[1,4]{1,0:T(1,128)S(1)} %get-tuple-element.11.means_ref), custom_call_target="tpu_custom_call" | custom-call | tf_op jit(solution)/shard_map/write_out/pallas_call | solution.py:520
